TPU v7x, 512 devices: a whole 4x4x16 slice. The times are simulated.
512 devices in a mesh: wide: 128 (over y, z, core), col: 4 (over x).
Axes of the slice: x: 4, y: 4, z: 16, core: 2. Of those that a mesh axis runs over, the one named last changes fastest.
Arguments:
- atom_feats: bfloat16 [65536, 128], P(('wide', 'col')), may hold values from -6 to 6
- atom_token: int32 [65536], P(('wide', 'col')), may hold values from 0 to 1023, as said below
- key_offset: int32 [2048], P(('wide', 'col')), may hold values from 0 to 32
- pair_in: bfloat16 [1024, 1024, 128], P('wide', 'col'), may hold values from -6 to 6
- w_qkv: bfloat16 [2, 128, 384], replicated, may hold values from -0.5 to 0.5
- w_out: bfloat16 [2, 128, 128], replicated, may hold values from -0.5 to 0.5
- w_up: bfloat16 [2, 128, 512], replicated, may hold values from -0.5 to 0.5
- w_down: bfloat16 [2, 256, 128], replicated, may hold values from -0.375 to 0.375
- w_tok: bfloat16 [128, 384], replicated, may hold values from -0.5 to 0.5
- w_row: bfloat16 [384, 128], replicated, may hold values from -0.3125 to 0.3125
- w_col: bfloat16 [384, 128], replicated, may hold values from -0.3125 to 0.3125
Outputs:
- atom_out: bfloat16 [65536, 128], P(('wide', 'col'))
- token_single: bfloat16 [1024, 384], P(('wide', 'col'))
- pair_out: bfloat16 [1024, 1024, 128], P('wide', 'col')
Inputs may be any that keep to these rules, and one draw needn't show every extreme that they name: atom_token never falls, every token holds one atom or more, and for every atom l, floor(l / 64) - 1 <= atom_token[l] <= floor(l / 64).
All inputs are finite; a program needn't handle non-finite values.
Results may differ from a plain program's by a relative error of at most 0.012.
Values may be sent and summed in bfloat16 or wider, within the bound.
A program may use at most 64 MiB of HBM per device.

v0:
```python
import jax
import jax.numpy as jnp
from jax import lax
from jax.sharding import PartitionSpec as P

HEADS = 4
HEAD = 32
QBLK = 32
KWIN = 128


def padded(cells, sides, width):
    for axis, dim in sides:
        count = lax.axis_size(axis)
        ends = count - 1
        head = lax.slice_in_dim(cells, 0, width, axis=dim)
        tail = lax.slice_in_dim(cells, cells.shape[dim] - width, cells.shape[dim], axis=dim)
        cells = jnp.concatenate(
            [
                lax.ppermute(tail, axis, [(i, (i + 1) % count) for i in range(ends)]),
                cells,
                lax.ppermute(head, axis, [((i + 1) % count, i) for i in range(ends)]),
            ],
            axis=dim,
        )
    return cells


def from_behind(value, axis, by):
    count = lax.axis_size(axis)
    pairs = [(i, i + by) for i in range(count) if 0 <= i + by < count]
    return lax.ppermute(value, axis, pairs)


def normalize(values):
    row_mean = jnp.mean(values, axis=-1, keepdims=True)
    centred = values - row_mean
    return centred * lax.rsqrt(jnp.mean(centred * centred, axis=-1, keepdims=True) + 1e-05)


def windows(queries, key_rows, value_rows, win_starts, key_valid):

    def take_window(start):
        return (
            lax.dynamic_slice_in_dim(key_rows, start, KWIN, 0),
            lax.dynamic_slice_in_dim(value_rows, start, KWIN, 0),
        )

    key_win, value_win = jax.vmap(take_window)(win_starts)
    block_count = win_starts.shape[0]
    query_four = queries.reshape(block_count, QBLK, HEADS, HEAD)
    key_four = key_win.reshape(block_count, KWIN, HEADS, HEAD)
    value_four = value_win.reshape(block_count, KWIN, HEADS, HEAD)
    scores = jnp.einsum(
        "bqhd,bkhd->bhqk", query_four, key_four, preferred_element_type=jnp.float32
    ) * (1.0 / HEAD**0.5)
    weights = jnp.exp(scores) * key_valid[:, None, None, :]
    weights = (weights / jnp.sum(weights, axis=-1, keepdims=True)).astype(jnp.bfloat16)
    attended = jnp.einsum(
        "bhqk,bkhd->bqhd", weights, value_four, preferred_element_type=jnp.float32
    )
    return attended.reshape(block_count * QBLK, HEADS * HEAD).astype(jnp.bfloat16)


def on_device(
    atom_feats, atom_token, key_offset, pair_in, w_qkv, w_out, w_up, w_down, w_tok, w_row, w_col
):
    atom_rows, feat_width = atom_feats.shape
    shards = lax.axis_size("wide") * lax.axis_size("col")
    anchor = lax.axis_index(("wide", "col")) * atom_rows
    rim_width = KWIN - 2 * QBLK
    block_ids = jnp.arange(atom_rows // QBLK, dtype=jnp.int32)
    win_starts = block_ids * QBLK + key_offset
    key_pos = (
        anchor + (win_starts - rim_width)[:, None] + jnp.arange(KWIN, dtype=jnp.int32)[None, :]
    )
    key_valid = ((key_pos >= 0) & (key_pos < shards * atom_rows)).astype(jnp.float32)
    hidden_state = atom_feats.astype(jnp.float32)
    for layer_idx in range(w_qkv.shape[0]):
        normed = normalize(hidden_state).astype(jnp.bfloat16)
        projected = jnp.dot(normed, w_qkv[layer_idx], preferred_element_type=jnp.float32).astype(
            jnp.bfloat16
        )
        queries = projected[:, :feat_width]
        key_vals = padded(projected[:, feat_width:], ((("wide", "col"), 0),), rim_width)
        attended = windows(
            queries, key_vals[:, :feat_width], key_vals[:, feat_width:], win_starts, key_valid
        )
        hidden_state = hidden_state + jnp.dot(
            attended, w_out[layer_idx], preferred_element_type=jnp.float32
        )
        normed = normalize(hidden_state).astype(jnp.bfloat16)
        hidden = jnp.dot(normed, w_up[layer_idx], preferred_element_type=jnp.float32)
        half_up = w_down.shape[1]
        gated_mid = (jax.nn.silu(hidden[:, :half_up]) * hidden[:, half_up:]).astype(jnp.bfloat16)
        hidden_state = hidden_state + jnp.dot(
            gated_mid, w_down[layer_idx], preferred_element_type=jnp.float32
        )
    atom_out = hidden_state.astype(jnp.bfloat16)
    tok_act = jax.nn.relu(jnp.dot(atom_out, w_tok, preferred_element_type=jnp.float32)).astype(
        jnp.bfloat16
    )
    tok_sub = pair_in.shape[0] // lax.axis_size("col")
    first_tok = lax.axis_index(("wide", "col")) * tok_sub - 1
    tok_ids = first_tok + jnp.arange(tok_sub + 1, dtype=jnp.int32)
    matches = atom_token[None, :] == tok_ids[:, None]
    partial_value = jnp.dot(
        matches.astype(jnp.bfloat16), tok_act, preferred_element_type=jnp.float32
    )
    part_counts = jnp.sum(matches.astype(jnp.float32), axis=1)
    spill_sums, spill_counts = from_behind(
        (partial_value[:1], part_counts[:1]), ("wide", "col"), -1
    )
    tail_mask = (jnp.arange(tok_sub, dtype=jnp.int32) == tok_sub - 1).astype(jnp.float32)
    tok_sums = partial_value[1:] + tail_mask[:, None] * spill_sums
    counts = part_counts[1:] + tail_mask * spill_counts
    token_single = (tok_sums / counts[:, None]).astype(jnp.bfloat16)
    row_proj = jnp.dot(token_single, w_row, preferred_element_type=jnp.float32).astype(jnp.bfloat16)
    col_proj = jnp.dot(token_single, w_col, preferred_element_type=jnp.float32).astype(jnp.bfloat16)
    row_vecs = lax.all_gather(row_proj, "col", axis=0, tiled=True)
    all_cols = lax.all_gather(col_proj, ("wide", "col"), axis=0, tiled=True)
    col_count = pair_in.shape[1]
    col_vecs = lax.dynamic_slice_in_dim(all_cols, lax.axis_index("col") * col_count, col_count, 0)
    summed = pair_in.astype(jnp.float32) + row_vecs[:, None, :].astype(jnp.float32)
    pair_out = (summed + col_vecs[None, :, :].astype(jnp.float32)).astype(jnp.bfloat16)
    return (atom_out, token_single, pair_out)


def solution(mesh):
    return jax.shard_map(
        on_device,
        mesh=mesh,
        in_specs=(
            P(("wide", "col"), None),
            P(("wide", "col")),
            P(("wide", "col")),
            P("wide", "col", None),
            P(),
            P(),
            P(),
            P(),
            P(),
            P(),
            P(),
        ),
        out_specs=(P(("wide", "col"), None), P(("wide", "col"), None), P("wide", "col", None)),
        check_vma=False,
    )
```

profile of v0, /device:TPU:8, one launch (start us, length us, event | category | flops | bytes accessed | tf_op | source)
XLA Modules:
  0.0 257.2 jit_solution(18431431356042609795)
XLA Ops:
  0.6 0.9 copy.45
  1.6 1.1 convolution_convert_fusion.3
  2.8 3.4 %collective-permute-start = (bf16[64,256]{1,0:T(8,128)(2,1)S(1)}, bf16[64,256]{1,0:T(8,128)(2,1)S(1)}, u32[]{:S(2)}, u32[]{:S(2)}) collective-permute-start(bf16[64,256]{1,0:T(8,128)(2,1)S(1)} %get-tuple-element.85), channel_id=1, source_target_pairs={{0,1},{1,2},{2,3},{3,4},{4,5},{5,6},{6,7},{7,8},{8,9},{9,10},{10,1... | collective-permute-start | bytes 98312 | tf_op jit(solution)/shard_map/ppermute | solution.py:20
  6.2 11.4 %collective-permute-start.1 = (bf16[64,256]{1,0:T(8,128)(2,1)S(1)}, bf16[64,256]{1,0:T(8,128)(2,1)S(1)}, u32[]{:S(2)}, u32[]{:S(2)}) collective-permute-start(bf16[64,256]{1,0:T(8,128)(2,1)S(1)} %get-tuple-element.86), channel_id=1, source_target_pairs={{1,0},{2,1},{3,2},{4,3},{5,4},{6,5},{7,6},{8,7},{9,8},{10,9},{11,1... | collective-permute-start | bytes 98312 | tf_op jit(solution)/shard_map/ppermute | solution.py:22
  18.5 3.5 %collective-permute-start.5 = (f32[1]{0:T(128)S(1)}, f32[1]{0:T(128)}, u32[]{:S(2)}, u32[]{:S(2)}) collective-permute-start(f32[1]{0:T(128)S(1)} %bitcast.97), channel_id=1, source_target_pairs={{1,0},{2,1},{3,2},{4,3},{5,4},{6,5},{7,6},{8,7},{9,8},{10,9},{11,1... | collective-permute-start | bytes 20 | tf_op jit(solution)/shard_map/ppermute | solution.py:32
  22.3 0.7 slice-done
  23.0 5.6 %while.5 = (s32[]{:T(128)}, bf16[256,128]{1,0:T(8,128)(2,1)S(1)}, s32[4,2]{0,1:T(2,128)S(1)}, bf16[4,128,128]{1,2,0:T(8,128)(2,1)S(1)}, s32[]{:T(128)}) while((s32[]{:T(128)}, bf16[256,128]{1,0:T(8,128)(2,1)S(1)}, s32[4,2]{0,1:T(2,128)S(1)}, bf16[4,128,128]{1,2,0:T(8,128)(2,1)S(1)}, s32[]{:T(128)}) %tuple.68), condition=%wide.while_cond.1, body=%wide.while_body.1.sunk | while | flops 2 | bytes 196705 | solution.py:45
  23.6 0.7 dynamic-slice_bitcast_fusion.9
  25.0 0.7 dynamic-slice_bitcast_fusion.9
  26.4 0.7 dynamic-slice_bitcast_fusion.9
  27.9 0.7 dynamic-slice_bitcast_fusion.9
  28.7 5.6 %while.4 = (s32[]{:T(128)}, bf16[256,128]{1,0:T(8,128)(2,1)S(1)}, s32[4,2]{0,1:T(2,128)S(1)}, bf16[4,128,128]{1,2,0:T(8,128)(2,1)S(1)}, s32[]{:T(128)}) while((s32[]{:T(128)}, bf16[256,128]{1,0:T(8,128)(2,1)S(1)}, s32[4,2]{0,1:T(2,128)S(1)}, bf16[4,128,128]{1,2,0:T(8,128)(2,1)S(1)}, s32[]{:T(128)}) %tuple.77), condition=%wide.while_cond, body=%wide.while_body.sunk | while | flops 2 | bytes 196705 | solution.py:46
  36.2 0.7 copy-done.11
  38.0 2.5 collective-permute-start.2
  40.5 7.3 %collective-permute-start.3 = (bf16[64,256]{1,0:T(8,128)(2,1)S(1)}, bf16[64,256]{1,0:T(8,128)(2,1)S(1)}, u32[]{:S(2)}, u32[]{:S(2)}) collective-permute-start(bf16[64,256]{1,0:T(8,128)(2,1)S(1)} %get-tuple-element.84), channel_id=1, source_target_pairs={{1,0},{2,1},{3,2},{4,3},{5,4},{6,5},{7,6},{8,7},{9,8},{10,9},{11,1... | collective-permute-start | bytes 98312 | tf_op jit(solution)/shard_map/ppermute | solution.py:22
  48.0 1.4 collective-permute-done.3
  49.4 5.6 %while.7 = (s32[]{:T(128)}, bf16[256,128]{1,0:T(8,128)(2,1)S(1)}, s32[4,2]{0,1:T(2,128)S(1)}, bf16[4,128,128]{1,2,0:T(8,128)(2,1)S(1)}, s32[]{:T(128)}) while((s32[]{:T(128)}, bf16[256,128]{1,0:T(8,128)(2,1)S(1)}, s32[4,2]{0,1:T(2,128)S(1)}, bf16[4,128,128]{1,2,0:T(8,128)(2,1)S(1)}, s32[]{:T(128)}) %tuple.78), condition=%wide.while_cond.3, body=%wide.while_body.3.sunk | while | flops 2 | bytes 196705 | solution.py:45
  55.1 5.6 %while.6 = (s32[]{:T(128)}, bf16[256,128]{1,0:T(8,128)(2,1)S(1)}, s32[4,2]{0,1:T(2,128)S(1)}, bf16[4,128,128]{1,2,0:T(8,128)(2,1)S(1)}, s32[]{:T(128)}) while((s32[]{:T(128)}, bf16[256,128]{1,0:T(8,128)(2,1)S(1)}, s32[4,2]{0,1:T(2,128)S(1)}, bf16[4,128,128]{1,2,0:T(8,128)(2,1)S(1)}, s32[]{:T(128)}) %tuple.79), condition=%wide.while_cond.2, body=%wide.while_body.2.sunk | while | flops 2 | bytes 196705 | solution.py:46
  62.6 7.9 %collective-permute-start.4 = (f32[1,384]{1,0:T(1,128)S(1)}, f32[1,384]{1,0:T(1,128)S(1)}, u32[]{:S(2)}, u32[]{:S(2)}) collective-permute-start(f32[1,384]{1,0:T(1,128)S(1)} %slice.177), channel_id=1, source_target_pairs={{1,0},{2,1},{3,2},{4,3},{5,4},{6,5},{7,6},{8,7},{9,8},{10,9},{11,1... | collective-permute-start | bytes 4616 | tf_op jit(solution)/shard_map/ppermute | solution.py:32
  70.5 0.8 fusion.63
  71.2 0.7 copy.55
  72.2 175.3 %all-gather.1 = bf16[512,2,128]{2,1,0:T(2,128)(2,1)S(1)} all-gather(bf16[1,2,128]{2,1,0:T(2,128)(2,1)S(1)} %fusion.10), channel_id=1, replica_groups=mesh['wide'=128,'col'=4] {'wide','col'}, dimensions={0}, use_global_device_ids=true | all-gather | bytes 262656 | tf_op jit(solution)/shard_map/all_gather | solution.py:121
  247.7 8.6 %all-gather = bf16[4,2,128]{2,1,0:T(2,128)(2,1)S(1)} all-gather(bf16[1,2,128]{2,1,0:T(2,128)(2,1)S(1)} %fusion.9), channel_id=1, replica_groups=mesh['wide'=128,'col'=4] {'col'}, dimensions={0}, use_global_device_ids=true | all-gather | bytes 2560 | tf_op jit(solution)/shard_map/all_gather | solution.py:120
  256.3 0.9 add_convert_fusion
  (165 shorter events, 25.8 us)
Async XLA Ops:
  0.6 61.6 %copy-start = (bf16[128,384]{1,0:T(8,128)(2,1)S(1)}, bf16[128,384]{1,0:T(8,128)(2,1)}, u32[]{:S(2)}) copy-start(bf16[128,384]{1,0:T(8,128)(2,1)} %param.19) | copy-start | bytes 294916
  2.8 19.3 %copy-start.1 = (bf16[128,384]{1,0:T(8,128)(2,1)}, bf16[128,384]{1,0:T(8,128)(2,1)S(1)}, u32[]{:S(2)}) copy-start(bf16[128,384]{1,0:T(8,128)(2,1)S(1)} %convolution_convert_fusion.3) | copy-start | bytes 294916
  2.8 19.5 %collective-permute-start = (bf16[64,256]{1,0:T(8,128)(2,1)S(1)}, bf16[64,256]{1,0:T(8,128)(2,1)S(1)}, u32[]{:S(2)}, u32[]{:S(2)}) collective-permute-start(bf16[64,256]{1,0:T(8,128)(2,1)S(1)} %get-tuple-element.85), channel_id=1, source_target_pairs={{0,1},{1,2},{2,3},{3,4},{4,5},{5,6},{6,7},{7,8},{8,9},{9,10},{10,1... | collective-permute-start | bytes 98312 | tf_op jit(solution)/shard_map/ppermute | solution.py:20
  6.2 16.1 %collective-permute-start.1 = (bf16[64,256]{1,0:T(8,128)(2,1)S(1)}, bf16[64,256]{1,0:T(8,128)(2,1)S(1)}, u32[]{:S(2)}, u32[]{:S(2)}) collective-permute-start(bf16[64,256]{1,0:T(8,128)(2,1)S(1)} %get-tuple-element.86), channel_id=1, source_target_pairs={{1,0},{2,1},{3,2},{4,3},{5,4},{6,5},{7,6},{8,7},{9,8},{10,9},{11,1... | collective-permute-start | bytes 98312 | tf_op jit(solution)/shard_map/ppermute | solution.py:22
  17.7 0.7 copy-start.12
  18.5 3.5 %copy-start.10 = (s32[4]{0:T(128)S(1)}, s32[4]{0:T(128)}, u32[]{:S(2)}) copy-start(s32[4]{0:T(128)} %param.13) | copy-start | bytes 52
  18.5 52.0 %collective-permute-start.5 = (f32[1]{0:T(128)S(1)}, f32[1]{0:T(128)}, u32[]{:S(2)}, u32[]{:S(2)}) collective-permute-start(f32[1]{0:T(128)S(1)} %bitcast.97), channel_id=1, source_target_pairs={{1,0},{2,1},{3,2},{4,3},{5,4},{6,5},{7,6},{8,7},{9,8},{10,9},{11,1... | collective-permute-start | bytes 20 | tf_op jit(solution)/shard_map/ppermute | solution.py:32
  22.1 0.8 slice-start
  34.8 0.8 copy-start.8
  34.9 1.0 copy-start.4
  35.9 0.9 copy-start.11
  36.8 0.9 copy-start.5
  38.0 9.8 %copy-start.2 = (bf16[128,384]{1,0:T(8,128)(2,1)}, bf16[128,384]{1,0:T(8,128)(2,1)S(1)}, u32[]{:S(2)}) copy-start(bf16[128,384]{1,0:T(8,128)(2,1)S(1)} %convolution_convert_fusion.2) | copy-start | bytes 294916
  38.0 10.0 %collective-permute-start.2 = (bf16[64,256]{1,0:T(8,128)(2,1)S(1)}, bf16[64,256]{1,0:T(8,128)(2,1)S(1)}, u32[]{:S(2)}, u32[]{:S(2)}) collective-permute-start(bf16[64,256]{1,0:T(8,128)(2,1)S(1)} %get-tuple-element.83), channel_id=1, source_target_pairs={{0,1},{1,2},{2,3},{3,4},{4,5},{5,6},{6,7},{7,8},{8,9},{9,10},{10,1... | collective-permute-start | bytes 98312 | tf_op jit(solution)/shard_map/ppermute | solution.py:20
  40.5 8.9 %collective-permute-start.3 = (bf16[64,256]{1,0:T(8,128)(2,1)S(1)}, bf16[64,256]{1,0:T(8,128)(2,1)S(1)}, u32[]{:S(2)}, u32[]{:S(2)}) collective-permute-start(bf16[64,256]{1,0:T(8,128)(2,1)S(1)} %get-tuple-element.84), channel_id=1, source_target_pairs={{1,0},{2,1},{3,2},{4,3},{5,4},{6,5},{7,6},{8,7},{9,8},{10,9},{11,1... | collective-permute-start | bytes 98312 | tf_op jit(solution)/shard_map/ppermute | solution.py:22
  47.8 1.5 slice-start.1
  62.0 10.1 %copy-start.6 = (bf16[384,128]{1,0:T(8,128)(2,1)S(1)}, bf16[384,128]{1,0:T(8,128)(2,1)}, u32[]{:S(2)}) copy-start(bf16[384,128]{1,0:T(8,128)(2,1)} %param.21) | copy-start | bytes 294916
  62.0 185.5 %copy-start.7 = (bf16[384,128]{1,0:T(8,128)(2,1)S(1)}, bf16[384,128]{1,0:T(8,128)(2,1)}, u32[]{:S(2)}) copy-start(bf16[384,128]{1,0:T(8,128)(2,1)} %param.20) | copy-start | bytes 294916
  62.3 194.0 %copy-start.3 = (bf16[8,256,128]{2,1,0:T(8,128)(2,1)S(1)}, bf16[8,256,128]{2,1,0:T(8,128)(2,1)}, u32[]{:S(2)}) copy-start(bf16[8,256,128]{2,1,0:T(8,128)(2,1)} %param.14) | copy-start | bytes 1572868
  62.6 9.4 %collective-permute-start.4 = (f32[1,384]{1,0:T(1,128)S(1)}, f32[1,384]{1,0:T(1,128)S(1)}, u32[]{:S(2)}, u32[]{:S(2)}) collective-permute-start(f32[1,384]{1,0:T(1,128)S(1)} %slice.177), channel_id=1, source_target_pairs={{1,0},{2,1},{3,2},{4,3},{5,4},{6,5},{7,6},{8,7},{9,8},{10,9},{11,1... | collective-permute-start | bytes 4616 | tf_op jit(solution)/shard_map/ppermute | solution.py:32
  72.1 175.4 %copy-start.9 = (bf16[2,384]{1,0:T(2,128)(2,1)}, bf16[2,384]{1,0:T(2,128)(2,1)S(1)}, u32[]{:S(2)}) copy-start(bf16[2,384]{1,0:T(2,128)(2,1)S(1)} %fusion.54) | copy-start | bytes 4612
where the time goes:
time: 258 us; the launch traced here: 257 us
  blocking collectives  184 us (71%)
  starting transfers between devices  36 us (14%)
  local copies, waits for them, and re-layouts  27.8 us (11%)
  matrix products  4.11 us (2%)
    all_gather x1, blocking collectives, on_device(): all_cols = lax.all_gather(col_proj, ('wide', 'col'), axis=0, tiled=True)  175 us
    gather x80, local copies, waits for them, and re-layouts  22 us
    ppermute x2, starting transfers between devices, padded(): lax.ppermute(head, axis, [((i + 1) % count, i) for i in range(ends)])  18.7 us
    ppermute x2, starting transfers between devices, from_behind(): return lax.ppermute(value, axis, pairs)  11.4 us
    all_gather x1, blocking collectives, on_device(): row_vecs = lax.all_gather(row_proj, 'col', axis=0, tiled=True)  8.63 us
    ppermute x2, starting transfers between devices, padded(): lax.ppermute(tail, axis, [(i, (i + 1) % count) for i in range(ends)])  5.88 us
  transfers between devices with their start and end apart: 6, of which 1 were waited for; matrix products, arithmetic and copies ran while one was open for 11% of the time, Pallas kernels for 0%

commit v1 on v0

v1 whole, which is shorter than its diff:
```python
import functools

import jax
import jax.numpy as jnp
from jax import lax
from jax.experimental import pallas as pl
from jax.experimental.pallas import tpu as pltpu
from jax.sharding import PartitionSpec as P

D = 128
HEADS = 4
HEAD = 32
FFH = 256
TOKC = 384
QBLK = 32
KWIN = 128
RIM = 64
ROWS = 128
NY, NZ, NX = 4, 16, 4
SPREAD = 2
GROUP = NZ // SPREAD
STEPS = [d for d in range(-(GROUP // 2) + 1, GROUP // 2 + 1) if d != 0]
SCORE = 1.4426950408889634 / HEAD**0.5
NEG = -1e30
MESH = pl.DeviceIdType.MESH
f32, bf16 = jnp.float32, jnp.bfloat16


def device(y, z, core, x):
    return ((y * NZ + z) * 2 + core, x)


def along(step):
    at = lax.rem(lax.axis_index("wide") * NX + lax.axis_index("col") + step + 512, 512)
    return (at // NX, lax.rem(at, NX))


def dot(a, b):
    return jnp.dot(a, b, preferred_element_type=f32)


def norm(v):
    c = v - jnp.mean(v, axis=-1, keepdims=True)
    return (c * lax.rsqrt(jnp.mean(c * c, axis=-1, keepdims=True) + 1e-5)).astype(bf16)


def window_bias(offsets, first_block, query_row, n_query, n_key, base, n_atoms):
    parts = []
    for k in range(n_query // QBLK):
        off = offsets[first_block + k] + float(k * QBLK)
        key = lax.broadcasted_iota(jnp.int32, (QBLK, n_key), 1)
        rel = key.astype(f32) - off
        seen = (rel >= 0.0) & (rel < float(KWIN))
        pos = key + (base + query_row - RIM)
        here = (pos >= 0) & (pos < n_atoms)
        q_at = base + query_row + k * QBLK
        outside = (q_at < 0) | (q_at >= n_atoms)
        seen = seen & (here | outside)
        parts.append(jnp.where(seen, 0.0, NEG))
    return jnp.concatenate(parts, axis=0)


def attend(q, k, v, bias):
    n = q.shape[0]
    lane = lax.broadcasted_iota(jnp.int32, (n, D), 1) // HEAD
    stacked = jnp.concatenate(
        [jnp.where(lane == h, q, jnp.zeros_like(q)) for h in range(HEADS)], axis=0
    )
    scores = lax.dot_general(stacked, k, (((1,), (1,)), ((), ())), preferred_element_type=f32)
    weights = []
    for h in range(HEADS):
        e = jnp.exp2(scores[h * n : (h + 1) * n] * SCORE + bias)
        weights.append((e / jnp.sum(e, axis=-1, keepdims=True)).astype(bf16))
    out = dot(jnp.concatenate(weights, axis=0), v)
    total = jnp.zeros((n, D), f32)
    for h in range(HEADS):
        total = jnp.where(lane == h, out[h * n : (h + 1) * n], total)
    return total.astype(bf16)


def block(state, groups, biases, wq, wo, wu, wd):
    proj = dot(norm(state), wq).astype(bf16)
    kept = []
    for (row, n), bias in zip(groups, biases):
        lo, hi = row - RIM, row + n + RIM
        kept.append(attend(proj[row : row + n, :D], proj[lo:hi, D : 2 * D], proj[lo:hi, 2 * D :], bias))
    first = groups[0][0]
    last = groups[-1][0] + groups[-1][1]
    state = state[first:last] + dot(jnp.concatenate(kept, axis=0), wo)
    hidden = dot(norm(state), wu)
    gate, up = hidden[:, :FFH], hidden[:, FFH:]
    gated = (0.5 * gate * (1.0 + jnp.tanh(0.5 * gate)) * up).astype(bf16)
    return state + dot(gated, wd)


def kernel(
    n_atoms,
    feats, tok, koff, w_qkv, w_out, w_up, w_down, w_tok, w_row, w_col,
    atom_out, single, rows_out, cols_out,
    halo, far, wq, wo, wu, wd, wt, wp, mine, rowbuf, col_a, asm, gbuf,
    wsem, hsend, hrecv, rsend, rrecv, asend, arecv, bsend, brecv,
):
    wide, x = lax.axis_index("wide"), lax.axis_index("col")
    core = lax.rem(wide, 2)
    z = lax.rem(wide // 2, NZ)
    y = wide // (2 * NZ)
    me = wide * NX + x
    residue = lax.rem(z, GROUP)
    slot_a = (z // GROUP) * 8 + core * 4 + x
    home = x == y

    own = pltpu.make_async_copy(feats, halo.at[1, pl.ds(0, ROWS)], wsem.at[0])
    own.start()
    loads = []
    for n, (src, dst) in enumerate(
        [(w_qkv, wq), (w_out, wo), (w_up, wu), (w_down, wd), (w_tok, wt),
         (w_row, wp.at[:, pl.ds(0, D)]), (w_col, wp.at[:, pl.ds(D, D)])]
    ):
        loads.append(pltpu.make_async_copy(src, dst, wsem.at[n + 1]))
        loads[-1].start()

    barrier = pltpu.get_barrier_semaphore()

    def greet(dev):
        pl.semaphore_signal(barrier, inc=1, device_id=dev, device_id_type=MESH)

    for step in (-1, 1, 2):
        greet(along(step))
    for d in range(1, NX):
        greet((wide, lax.rem(x + d, NX)))
    for k in range(SPREAD):
        for c in range(2):
            for xs in range(NX):
                self_case = (home & (core == c) & (xs == x)) if k == 0 else None
                dev = device(x, lax.rem(z + k * GROUP, NZ), c, xs)
                if self_case is None:
                    greet(dev)
                else:
                    pl.when(jnp.logical_not(self_case))(functools.partial(greet, dev))
    for d in STEPS:
        greet(device(y, lax.rem(z - d + NZ, NZ), core, x))

    lanes = lax.broadcasted_iota(jnp.int32, (16, D), 0)
    tok_rel = (tok[...] - 2 * me).astype(f32)
    off4 = koff[...].astype(f32)
    offs = jnp.concatenate([off4] + [jnp.zeros((1, 4), f32)] * (D // 4 - 1), axis=1)
    meta = jnp.where(lanes == 0, tok_rel, jnp.where(lanes == 1, offs, 0.0))
    halo[1, pl.ds(ROWS, 16)] = meta.astype(bf16)
    own.wait()
    pl.semaphore_wait(barrier, 3 + 3 + 8 * SPREAD + len(STEPS) - home.astype(jnp.int32))

    sends = [
        pltpu.make_async_remote_copy(halo.at[1], halo.at[0], hsend.at[0], hrecv.at[0], along(1), MESH),
        pltpu.make_async_remote_copy(halo.at[1], halo.at[2], hsend.at[1], hrecv.at[1], along(-1), MESH),
        pltpu.make_async_remote_copy(
            halo.at[1, pl.ds(0, RIM)], far, hsend.at[2], hrecv.at[2], along(-2), MESH
        ),
    ]
    for s in sends:
        s.start()
    for load in loads:
        load.wait()
    for s in sends:
        s.wait_recv()

    metas = [halo[s, pl.ds(ROWS, 16)].astype(f32) for s in range(3)]
    offsets = [m[1:2, b : b + 1] for m in metas for b in range(4)]
    base = me * ROWS - ROWS
    spans1 = [(64, 128), (192, 128), (320, 64)]
    bias1 = [
        window_bias(offsets, row // QBLK, row, n, n + 2 * RIM, base, n_atoms) for row, n in spans1
    ]
    spans2 = [(64, 128), (192, 64)]
    bias2 = [
        window_bias(offsets, row // QBLK + 2, row, n, n + 2 * RIM, base + RIM, n_atoms)
        for row, n in spans2
    ]
    state = jnp.concatenate(
        [halo[0, pl.ds(0, ROWS)], halo[1, pl.ds(0, ROWS)], halo[2, pl.ds(0, ROWS)], far[...]], axis=0
    ).astype(f32)
    state = block(state, spans1, bias1, wq[0], wo[0], wu[0], wd[0])
    state = block(state, spans2, bias2, wq[1], wo[1], wu[1], wd[1])
    atoms = state.astype(bf16)
    atom_out[...] = atoms[:ROWS]

    act = jnp.maximum(dot(atoms, wt[...]), 0.0).astype(bf16)
    rel = jnp.concatenate([metas[1][0:1, :], metas[2][0:1, :RIM] + 2.0], axis=1)
    match = jnp.where(
        lax.broadcasted_iota(jnp.int32, (16, ROWS + RIM), 0).astype(f32) == rel, 1.0, 0.0
    )
    counts = jnp.maximum(jnp.sum(match, axis=-1, keepdims=True), 1.0)
    means = (dot(match.astype(bf16), act) / counts).astype(bf16)
    single[...] = means[0:2]
    proj = dot(means, wp[...]).astype(bf16).astype(f32)
    mine[0] = proj[0:2, :D]
    mine[1] = proj[0:2, D:]
    rowbuf[pl.ds(x, 1)] = proj[0:2, :D].reshape(1, 2, D)

    for k in range(SPREAD):
        zd = lax.rem(z + k * GROUP, NZ)
        for yd in range(NY):
            for c in range(2):
                def send_a(zd=zd, yd=yd, c=c):
                    pltpu.make_async_remote_copy(
                        mine.at[1], col_a.at[slot_a], asend, arecv, device(yd, zd, c, y), MESH
                    ).start()
                if k == 0:
                    self_case = home & (core == c) & (y == yd)
                    pl.when(jnp.logical_not(self_case))(send_a)
                else:
                    send_a()
    own_a = pltpu.make_async_copy(mine.at[1], col_a.at[slot_a], arecv)
    pl.when(home)(own_a.start)
    for d in range(1, NX):
        pltpu.make_async_remote_copy(
            mine.at[0], rowbuf.at[x], rsend, rrecv, (wide, lax.rem(x + d, NX)), MESH
        ).start()
    pltpu.make_async_copy(col_a, col_a, arecv).wait()

    for s in range(8 * SPREAD):
        asm[pl.ds(2 * s, 2), :] = col_a[s]
    gbuf[pl.ds(residue, 1)] = asm[...].astype(bf16).reshape(1, 16 * SPREAD, D)

    for d in STEPS:
        pltpu.make_async_remote_copy(
            gbuf.at[residue], gbuf.at[residue], bsend, brecv,
            device(y, lax.rem(z + d + NZ, NZ), core, x), MESH,
        ).start()
    rest = gbuf.at[pl.ds(0, len(STEPS))]
    pltpu.make_async_copy(rowbuf.at[pl.ds(0, 3)], rowbuf.at[pl.ds(0, 3)], rrecv).wait()
    for s in range(NX):
        rows_out[pl.ds(2 * s, 2), :] = rowbuf[s]
    pltpu.make_async_copy(rest, rest, brecv).wait()
    for r in range(GROUP):
        for k in range(SPREAD):
            cols_out[pl.ds((k * GROUP + r) * 16, 16), :] = gbuf[r, pl.ds(16 * k, 16)]

    for s in sends:
        s.wait_send()
    pltpu.make_async_copy(rowbuf.at[pl.ds(0, 3)], rowbuf.at[pl.ds(0, 3)], rsend).wait()
    less = col_a.at[pl.ds(0, 8 * SPREAD - 1)]
    pl.when(home)(pltpu.make_async_copy(less, less, asend).wait)
    pl.when(jnp.logical_not(home))(pltpu.make_async_copy(col_a, col_a, asend).wait)
    pltpu.make_async_copy(rest, rest, bsend).wait()


def on_device(
    atom_feats, atom_token, key_offset, pair_in, w_qkv, w_out, w_up, w_down, w_tok, w_row, w_col
):
    vmem = pl.BlockSpec(memory_space=pltpu.VMEM)
    hbm = pl.BlockSpec(memory_space=pl.ANY)
    dma = pltpu.SemaphoreType.DMA
    atom_out, single, row_vecs, col_vecs = pl.pallas_call(
        functools.partial(kernel, 512 * ROWS),
        out_shape=[
            jax.ShapeDtypeStruct((ROWS, D), bf16),
            jax.ShapeDtypeStruct((2, TOKC), bf16),
            jax.ShapeDtypeStruct((8, D), f32),
            jax.ShapeDtypeStruct((256, D), bf16),
        ],
        in_specs=[hbm, vmem, vmem] + [hbm] * 7,
        out_specs=[vmem] * 4,
        scratch_shapes=[
            pltpu.VMEM((3, ROWS + 16, D), bf16),
            pltpu.VMEM((RIM, D), bf16),
            pltpu.VMEM((2, D, 3 * D), bf16),
            pltpu.VMEM((2, D, D), bf16),
            pltpu.VMEM((2, D, 2 * FFH), bf16),
            pltpu.VMEM((2, FFH, D), bf16),
            pltpu.VMEM((D, TOKC), bf16),
            pltpu.VMEM((TOKC, 2 * D), bf16),
            pltpu.VMEM((2, 2, D), f32),
            pltpu.VMEM((NX, 2, D), f32),
            pltpu.VMEM((8 * SPREAD, 2, D), f32),
            pltpu.VMEM((16 * SPREAD, D), f32),
            pltpu.VMEM((GROUP, 16 * SPREAD, D), bf16),
            dma((8,)), dma((3,)), dma((3,)), dma, dma, dma, dma, dma, dma,
        ],
        compiler_params=pltpu.CompilerParams(
            collective_id=1, has_side_effects=True, vmem_limit_bytes=32 * 1024 * 1024
        ),
        name="atoms_tokens",
    )(
        atom_feats, atom_token.reshape(1, ROWS), key_offset.reshape(1, 4),
        w_qkv, w_out, w_up, w_down, w_tok, w_row, w_col,
    )
    summed = pair_in.astype(f32) + row_vecs[:, None, :]
    pair_out = (summed + col_vecs[None, :, :].astype(f32)).astype(bf16)
    return (atom_out, single, pair_out)


def solution(mesh):
    return jax.shard_map(
        on_device,
        mesh=mesh,
        in_specs=(
            P(("wide", "col"), None),
            P(("wide", "col")),
            P(("wide", "col")),
            P("wide", "col", None),
            P(), P(), P(), P(), P(), P(), P(),
        ),
        out_specs=(P(("wide", "col"), None), P(("wide", "col"), None), P("wide", "col", None)),
        check_vma=False,
    )
```

time: 258 us -> 51.1 us (0.20)
  the two profiles are of different devices: /device:TPU:8 before, /device:TPU:2 now
where the time goes in v1:
time: 51.1 us; the launch traced here: 50.7 us
  Pallas kernels  40.2 us (79%)
  local copies, waits for them, and re-layouts  8.89 us (17%)
  other arithmetic  0.94 us (2%)
  between operations  0.69 us (1%)
    pallas_call x1, Pallas kernels, on_device(): pl.pallas_call(functools.partial(kernel, 512 * ROWS), out_shape=[jax.Shap...  40.2 us
    unnamed x24, local copies, waits for them, and re-layouts  8.89 us

profile of v1, /device:TPU:2, one launch (start us, length us, event | category | flops | bytes accessed | tf_op | source)
XLA Modules:
  0.0 50.7 jit_solution(8515562305076646838)
XLA Ops:
  0.6 0.0 copy-start.8
  0.6 0.0 copy-start.9
  0.7 0.6 %copy-done.8 = s32[128]{0:T(128)S(1)} copy-done((s32[128]{0:T(128)S(1)}, s32[128]{0:T(128)}, u32[]{:S(2)}) %copy-start.8) | copy-done | bytes 536
  1.3 0.0 copy-done.9
  1.3 0.9 %copy-done = bf16[2,128,512]{2,1,0:T(8,128)(2,1)S(1)} copy-done((bf16[2,128,512]{2,1,0:T(8,128)(2,1)S(1)}, bf16[2,128,512]{2,1,0:T(8,128)(2,1)}, u32[]{:S(2)}) %copy-start) | copy-done | bytes 262168
  2.3 0.0 copy-start.1
  2.3 0.9 %copy-done.1 = bf16[2,128,384]{2,1,0:T(8,128)(2,1)S(1)} copy-done((bf16[2,128,384]{2,1,0:T(8,128)(2,1)S(1)}, bf16[2,128,384]{2,1,0:T(8,128)(2,1)}, u32[]{:S(2)}) %copy-start.1) | copy-done | bytes 196632
  3.2 0.0 copy-start.2
  3.2 0.9 %copy-done.2 = bf16[2,256,128]{2,1,0:T(8,128)(2,1)S(1)} copy-done((bf16[2,256,128]{2,1,0:T(8,128)(2,1)S(1)}, bf16[2,256,128]{2,1,0:T(8,128)(2,1)}, u32[]{:S(2)}) %copy-start.2) | copy-done | bytes 131096
  4.1 0.0 copy-start.3
  4.1 0.9 %copy-done.3 = bf16[128,384]{1,0:T(8,128)(2,1)S(1)} copy-done((bf16[128,384]{1,0:T(8,128)(2,1)S(1)}, bf16[128,384]{1,0:T(8,128)(2,1)}, u32[]{:S(2)}) %copy-start.3) | copy-done | bytes 98328
  5.0 0.0 copy-start.4
  5.0 0.9 %copy-done.4 = bf16[384,128]{1,0:T(8,128)(2,1)S(1)} copy-done((bf16[384,128]{1,0:T(8,128)(2,1)S(1)}, bf16[384,128]{1,0:T(8,128)(2,1)}, u32[]{:S(2)}) %copy-start.4) | copy-done | bytes 98328
  5.9 0.0 copy-start.5
  5.9 0.9 %copy-done.5 = bf16[384,128]{1,0:T(8,128)(2,1)S(1)} copy-done((bf16[384,128]{1,0:T(8,128)(2,1)S(1)}, bf16[384,128]{1,0:T(8,128)(2,1)}, u32[]{:S(2)}) %copy-start.5) | copy-done | bytes 98328
  6.8 0.0 copy-start.6
  6.8 0.8 %copy-done.6 = bf16[2,128,128]{2,1,0:T(8,128)(2,1)S(1)} copy-done((bf16[2,128,128]{2,1,0:T(8,128)(2,1)S(1)}, bf16[2,128,128]{2,1,0:T(8,128)(2,1)}, u32[]{:S(2)}) %copy-start.6) | copy-done | bytes 65560
  7.6 0.0 copy-start.7
  7.6 0.8 %copy-done.7 = bf16[128,128]{1,0:T(8,128)(2,1)S(1)} copy-done((bf16[128,128]{1,0:T(8,128)(2,1)S(1)}, bf16[128,128]{1,0:T(8,128)(2,1)}, u32[]{:S(2)}) %copy-start.7) | copy-done | bytes 32792
  8.4 40.2 %atoms_tokens.1 = (bf16[128,128]{1,0:T(8,128)(2,1)S(1)}, bf16[2,384]{1,0:T(2,128)(2,1)S(1)}, f32[8,128]{1,0:T(8,128)S(1)}, bf16[256,128]{1,0:T(8,128)(2,1)S(1)}) custom-call(bf16[128,128]{1,0:T(8,128)(2,1)S(1)} %copy-done.7, s32[1,128]{1,0:T(1,128)S(1)} %bitcast.2, s32[1,4]{1,0:T(1,128)S(1)} %bitcast.3, bf16[2,128,384]{2,1,0:T(8,128)(2,1)S(1)} %copy-done.1, ...), custom_call_target="tpu_custom_call" | custom-call | tf_op jit(solution)/shard_map/atoms_tokens/pallas_call | solution.py:253
  48.6 0.0 copy-done.10
  48.6 0.9 %add_convert_fusion = bf16[8,256,128]{2,1,0:T(8,128)(2,1)} fusion(bf16[8,256,128]{2,1,0:T(8,128)(2,1)S(1)} %copy-done.10, f32[256,128]{1,0:T(8,128)S(1)} %convert_element_type.11, f32[8,128]{1,0:T(8,128)S(1)} %get-tuple-element.9), kind=kLoop, calls=%fused_computation | loop fusion | flops 1048576 | bytes 1183744 | tf_op jit(solution)/shard_map/convert_element_type | solution.py:288
  49.5 0.6 %copy.16 = bf16[128,128]{1,0:T(8,128)(2,1)} copy(bf16[128,128]{1,0:T(8,128)(2,1)S(1)} %get-tuple-element.14) | data formatting | bytes 65536
  50.1 0.6 %copy.17 = bf16[2,384]{1,0:T(2,128)(2,1)} copy(bf16[2,384]{1,0:T(2,128)(2,1)S(1)} %get-tuple-element.15) | data formatting | bytes 3072
  (3 shorter events, 0.0 us)
Async XLA Ops:
  0.6 0.7 %copy-start.8 = (s32[128]{0:T(128)S(1)}, s32[128]{0:T(128)}, u32[]{:S(2)}) copy-start(s32[128]{0:T(128)} %param.12) | copy-start | bytes 1540
  0.6 0.7 %copy-start.9 = (s32[4]{0:T(128)S(1)}, s32[4]{0:T(128)}, u32[]{:S(2)}) copy-start(s32[4]{0:T(128)} %param.13) | copy-start | bytes 52
  1.3 0.9 %copy-start = (bf16[2,128,512]{2,1,0:T(8,128)(2,1)S(1)}, bf16[2,128,512]{2,1,0:T(8,128)(2,1)}, u32[]{:S(2)}) copy-start(bf16[2,128,512]{2,1,0:T(8,128)(2,1)} %w_up.1) | copy-start | bytes 786436
  2.3 0.9 %copy-start.1 = (bf16[2,128,384]{2,1,0:T(8,128)(2,1)S(1)}, bf16[2,128,384]{2,1,0:T(8,128)(2,1)}, u32[]{:S(2)}) copy-start(bf16[2,128,384]{2,1,0:T(8,128)(2,1)} %w_qkv.1) | copy-start | bytes 589828
  3.2 0.9 %copy-start.2 = (bf16[2,256,128]{2,1,0:T(8,128)(2,1)S(1)}, bf16[2,256,128]{2,1,0:T(8,128)(2,1)}, u32[]{:S(2)}) copy-start(bf16[2,256,128]{2,1,0:T(8,128)(2,1)} %w_down.1) | copy-start | bytes 393220
  4.1 0.9 %copy-start.3 = (bf16[128,384]{1,0:T(8,128)(2,1)S(1)}, bf16[128,384]{1,0:T(8,128)(2,1)}, u32[]{:S(2)}) copy-start(bf16[128,384]{1,0:T(8,128)(2,1)} %w_tok.1) | copy-start | bytes 294916
  5.0 0.9 %copy-start.4 = (bf16[384,128]{1,0:T(8,128)(2,1)S(1)}, bf16[384,128]{1,0:T(8,128)(2,1)}, u32[]{:S(2)}) copy-start(bf16[384,128]{1,0:T(8,128)(2,1)} %w_row.1) | copy-start | bytes 294916
  5.9 0.9 %copy-start.5 = (bf16[384,128]{1,0:T(8,128)(2,1)S(1)}, bf16[384,128]{1,0:T(8,128)(2,1)}, u32[]{:S(2)}) copy-start(bf16[384,128]{1,0:T(8,128)(2,1)} %w_col.1) | copy-start | bytes 294916
  6.8 0.8 %copy-start.6 = (bf16[2,128,128]{2,1,0:T(8,128)(2,1)S(1)}, bf16[2,128,128]{2,1,0:T(8,128)(2,1)}, u32[]{:S(2)}) copy-start(bf16[2,128,128]{2,1,0:T(8,128)(2,1)} %w_out.1) | copy-start | bytes 196612
  7.6 0.8 %copy-start.7 = (bf16[128,128]{1,0:T(8,128)(2,1)S(1)}, bf16[128,128]{1,0:T(8,128)(2,1)}, u32[]{:S(2)}) copy-start(bf16[128,128]{1,0:T(8,128)(2,1)} %feats.1) | copy-start | bytes 98308
  8.4 40.2 %copy-start.10 = (bf16[8,256,128]{2,1,0:T(8,128)(2,1)S(1)}, bf16[8,256,128]{2,1,0:T(8,128)(2,1)}, u32[]{:S(2)}) copy-start(bf16[8,256,128]{2,1,0:T(8,128)(2,1)} %param.14) | copy-start | bytes 1572868

commit v2 on v1

v2 whole, which is shorter than its diff:
```python
import functools

import jax
import jax.numpy as jnp
from jax import lax
from jax.experimental import pallas as pl
from jax.experimental.pallas import tpu as pltpu
from jax.sharding import PartitionSpec as P

D = 128
HEADS = 4
HEAD = 32
FFH = 256
TOKC = 384
QBLK = 32
KWIN = 128
RIM = 64
ROWS = 128
NY, NZ, NX = 4, 16, 4
NEAR = (4, -4, 3, -3, 2, -2, 1, -1)
SCORE = 1.4426950408889634 / HEAD**0.5
NEG = -1e30
MESH = pl.DeviceIdType.MESH
f32, bf16 = jnp.float32, jnp.bfloat16


def device(y, z, core, x):
    return ((y * NZ + z) * 2 + core, x)


def along(step):
    at = lax.rem(lax.axis_index("wide") * NX + lax.axis_index("col") + step + 512, 512)
    return (at // NX, lax.rem(at, NX))


def dot(a, b):
    return jnp.dot(a, b, preferred_element_type=f32)


def norm(v):
    c = v - jnp.mean(v, axis=-1, keepdims=True)
    return (c * lax.rsqrt(jnp.mean(c * c, axis=-1, keepdims=True) + 1e-5)).astype(bf16)


def window_bias(offset, block, base, n_key, n_atoms):
    first = base - RIM
    at = base + block * QBLK
    outside = (at < 0) | (at >= n_atoms)
    floor = jnp.where(outside, -KWIN * 8, -first).astype(f32)
    ceil = jnp.where(outside, KWIN * 8, n_atoms - first).astype(f32)
    low = jnp.maximum(offset + float(block * QBLK), floor)
    high = jnp.minimum(offset + float(block * QBLK + KWIN), ceil)
    key = lax.broadcasted_iota(jnp.int32, (1, n_key), 1).astype(f32)
    return jnp.where((key >= low) & (key < high), 0.0, NEG)


def rows_of(blocks, n_key):
    return jnp.concatenate([jnp.broadcast_to(b[:, :n_key], (QBLK, n_key)) for b in blocks], axis=0)


def attend(q, k, v, bias):
    n = q.shape[0]
    lane = lax.broadcasted_iota(jnp.int32, (n, D), 1) // HEAD
    stacked = jnp.concatenate(
        [jnp.where(lane == h, q, jnp.zeros_like(q)) for h in range(HEADS)], axis=0
    )
    scores = lax.dot_general(stacked, k, (((1,), (1,)), ((), ())), preferred_element_type=f32)
    weights = []
    for h in range(HEADS):
        e = jnp.exp2(scores[h * n : (h + 1) * n] * SCORE + bias)
        weights.append((e / jnp.sum(e, axis=-1, keepdims=True)).astype(bf16))
    out = dot(jnp.concatenate(weights, axis=0), v)
    total = jnp.zeros((n, D), f32)
    for h in range(HEADS):
        total = jnp.where(lane == h, out[h * n : (h + 1) * n], total)
    return total.astype(bf16)


def block(state, proj, spans, biases, wo, wu, wd):
    kept = []
    for (row, n), bias in zip(spans, biases):
        lo, hi = row - RIM, row + n + RIM
        kept.append(
            attend(proj[row : row + n, :D], proj[lo:hi, D : 2 * D], proj[lo:hi, 2 * D :], bias)
        )
    first = spans[0][0]
    last = spans[-1][0] + spans[-1][1]
    state = state[first:last] + dot(jnp.concatenate(kept, axis=0), wo)
    hidden = dot(norm(state), wu)
    gate, up = hidden[:, :FFH], hidden[:, FFH:]
    gated = (0.5 * gate * (1.0 + jnp.tanh(0.5 * gate)) * up).astype(bf16)
    return state + dot(gated, wd)


def project(rows, wq):
    return dot(norm(rows), wq).astype(bf16)


def tokens(atoms, match, counts, wt, wp):
    act = jnp.maximum(dot(atoms, wt), 0.0).astype(bf16)
    means = (dot(match, act) / counts).astype(bf16)
    return means, dot(means, wp).astype(bf16)


def matches(own_meta, right_meta):
    rel = jnp.concatenate([own_meta[0:1, :], right_meta[0:1, :RIM] + 2.0], axis=1)
    ids = lax.broadcasted_iota(jnp.int32, (16, ROWS + RIM), 0).astype(f32)
    match = jnp.where(ids == rel, 1.0, 0.0)
    return match.astype(bf16), jnp.maximum(jnp.sum(match, axis=-1, keepdims=True), 1.0)


def biases_of(metas, base, n_atoms):
    out = []
    for start, n, n_key in ((-RIM, RIM, 192), (0, ROWS, 256), (ROWS, ROWS, 256)):
        span = []
        for k in range(n // QBLK):
            at = (start + ROWS) // QBLK + k
            off = metas[at // 4][1:2, at % 4 : at % 4 + 1]
            span.append(window_bias(off, k, base + start, n_key, n_atoms))
        out.append(span)
    return out


SPANS1 = [(64, 64), (128, 128), (256, 128)]
SPANS2 = [(64, 128), (192, 64)]


def transform(pieces, own_proj, metas, base, n_atoms, wq, wo, wu, wd):
    left, own, right, far = pieces
    biases = biases_of(metas, base, n_atoms)
    rim = project(jnp.concatenate([left, right, far], axis=0), wq[0])
    proj = jnp.concatenate([rim[:ROWS], own_proj, rim[ROWS:]], axis=0)
    state = jnp.concatenate([left, own, right, far], axis=0)
    bias1 = [rows_of(biases[0], 192), rows_of(biases[1], 256), rows_of(biases[2], 256)]
    state = block(state, proj, SPANS1, bias1, wo[0], wu[0], wd[0])
    bias2 = [bias1[1], rows_of(biases[2][:2], 192)]
    proj = project(state, wq[1])
    return block(state, proj, SPANS2, bias2, wo[1], wu[1], wd[1])


def peers():
    every = [(dy, dz, dc) for dy in range(NY) for dz in range(-7, 9) for dc in range(2)]
    return sorted(every, key=lambda o: (-(min(o[0], NY - o[0]) + abs(o[1])), -o[2]))


def kernel(
    n_atoms,
    feats, tok, koff, w_qkv, w_out, w_up, w_down, w_tok, w_row, w_col,
    atom_out, single, rows_out, cols_out,
    halo, far, toks, offs, wq, wo, wu, wd, wt, wp, mine, rowbuf, colbuf,
    wsem, hsend, hrecv, rsend, rrecv, csend, crecv, around, beyond,
):
    wide, x = lax.axis_index("wide"), lax.axis_index("col")
    core = lax.rem(wide, 2)
    z = lax.rem(wide // 2, NZ)
    y = wide // (2 * NZ)
    me = wide * NX + x
    home = x == y

    loads = []
    for n, (src, dst) in enumerate(
        [(feats, halo.at[1, pl.ds(0, ROWS)]), (tok, toks), (koff, offs),
         (w_qkv, wq), (w_out, wo), (w_up, wu), (w_down, wd), (w_tok, wt),
         (w_row, wp.at[:, pl.ds(0, D)]), (w_col, wp.at[:, pl.ds(D, D)])]
    ):
        loads.append(pltpu.make_async_copy(src, dst, wsem.at[n]))
        loads[-1].start()

    def tell(sem, dev):
        pl.semaphore_signal(sem, inc=1, device_id=dev, device_id_type=MESH)

    def beside(d):
        return device(y, lax.rem(z + d + NZ, NZ), core, x)

    barrier = pltpu.get_barrier_semaphore()
    for step in (-1, 1, 2):
        tell(barrier, along(step))
    for dy in range(NY):
        for dx in range(NX):
            for dc in range(2):
                if dy or dx or dc:
                    tell(
                        barrier,
                        device(lax.rem(y + dy, NY), z, lax.rem(core + dc, 2), lax.rem(x + dx, NX)),
                    )
    for d in NEAR:
        tell(barrier, beside(d))

    for load in loads[:3]:
        load.wait()
    row = lax.broadcasted_iota(jnp.int32, (16, D), 0)
    tok_rel = (toks[...] - 2 * me).astype(f32)
    off4 = jnp.concatenate(
        [offs[...].astype(f32)] + [jnp.zeros((1, 4), f32)] * (D // 4 - 1), axis=1
    )
    meta = jnp.where(row == 0, tok_rel, jnp.where(row == 1, off4, 0.0))
    halo[1, pl.ds(ROWS, 16)] = meta.astype(bf16)
    pl.semaphore_wait(barrier, 3 + 31 + len(NEAR))

    sends = [
        pltpu.make_async_remote_copy(
            halo.at[1], halo.at[0], hsend.at[0], hrecv.at[0], along(1), MESH
        ),
        pltpu.make_async_remote_copy(
            halo.at[1], halo.at[2], hsend.at[1], hrecv.at[1], along(-1), MESH
        ),
        pltpu.make_async_remote_copy(
            halo.at[1, pl.ds(0, RIM)], far, hsend.at[2], hrecv.at[2], along(-2), MESH
        ),
    ]
    for s in sends:
        s.start()

    for d in NEAR:
        tell(around, beside(d))
    loads[3].wait()
    own = halo[1, pl.ds(0, ROWS)].astype(f32)
    own_proj = project(own, wq[0])
    for load in loads[4:]:
        load.wait()
    for s in sends:
        s.wait_recv()
    pl.semaphore_wait(around, len(NEAR))
    for d in (4, -4):
        tell(beyond, beside(d))

    metas = [halo[s, pl.ds(ROWS, 16)].astype(f32) for s in range(3)]
    pieces = [halo[0, pl.ds(0, ROWS)].astype(f32), own]
    pieces += [halo[2, pl.ds(0, ROWS)].astype(f32), far[...].astype(f32)]
    match, counts = matches(metas[1], metas[2])
    state = transform(pieces, own_proj, metas, me * ROWS, n_atoms, wq, wo, wu, wd)
    atoms = state.astype(bf16)
    means, proj = tokens(atoms, match, counts, wt[...], wp[...])
    mine[0] = proj[0:2, :D]
    mine[1] = proj[0:2, D:]
    pl.semaphore_wait(beyond, 2)

    def send_column(dy, dz, dc):
        to = device(
            lax.rem(y + dy, NY), lax.rem(z + dz + NZ, NZ), lax.rem(core + dc, 2), y
        )
        pltpu.make_async_remote_copy(
            mine.at[1], colbuf.at[wide % 32 * NX + x], csend, crecv, to, MESH
        ).start()

    for dy, dz, dc in peers()[:-1]:
        send_column(dy, dz, dc)
    pl.when(jnp.logical_not(home))(functools.partial(send_column, 0, 0, 0))
    pl.when(home)(
        pltpu.make_async_copy(mine.at[1], colbuf.at[wide % 32 * NX + x], crecv).start
    )
    for d in range(1, NX):
        pltpu.make_async_remote_copy(
            mine.at[0], rowbuf.at[x], rsend, rrecv, (wide, lax.rem(x + d, NX)), MESH
        ).start()
    rowbuf[pl.ds(x, 1)] = proj[0:2, :D].reshape(1, 2, D)
    atom_out[...] = atoms[:ROWS]
    single[...] = means[0:2]

    three = rowbuf.at[pl.ds(0, 3)]
    pltpu.make_async_copy(three, three, rrecv).wait()
    for s in range(NX):
        rows_out[pl.ds(2 * s, 2), :] = rowbuf[s].astype(f32)
    for s in sends:
        s.wait_send()
    pltpu.make_async_copy(three, three, rsend).wait()
    less = colbuf.at[pl.ds(0, 127)]
    pl.when(home)(pltpu.make_async_copy(less, less, csend).wait)
    pl.when(jnp.logical_not(home))(pltpu.make_async_copy(colbuf, colbuf, csend).wait)
    pltpu.make_async_copy(colbuf, colbuf, crecv).wait()
    for s in range(128):
        cols_out[pl.ds(2 * s, 2), :] = colbuf[s].astype(f32)


def finish(pair, rows, cols, atoms, means, pair_out, atom_out, single, sums, sem):
    copies = [
        pltpu.make_async_copy(atoms, atom_out, sem.at[0]),
        pltpu.make_async_copy(means, single, sem.at[1]),
    ]
    for copy in copies:
        copy.start()
    cols = cols[...]
    for r in range(8):
        sums[r] = ((pair[r].astype(f32) + rows[pl.ds(r, 1), :]) + cols).astype(bf16)
        copies.append(pltpu.make_async_copy(sums.at[r], pair_out.at[r], sem.at[r + 2]))
        copies[-1].start()
    for copy in copies:
        copy.wait()


def on_device(
    atom_feats, atom_token, key_offset, pair_in, w_qkv, w_out, w_up, w_down, w_tok, w_row, w_col
):
    vmem = pl.BlockSpec(memory_space=pltpu.VMEM)
    hbm = pl.BlockSpec(memory_space=pltpu.HBM)
    dma, flag = pltpu.SemaphoreType.DMA, pltpu.SemaphoreType.REGULAR
    atoms, means, row_vecs, col_vecs = pl.pallas_call(
        functools.partial(kernel, 512 * ROWS),
        out_shape=[
            jax.ShapeDtypeStruct((ROWS, D), bf16),
            jax.ShapeDtypeStruct((2, TOKC), bf16),
            jax.ShapeDtypeStruct((8, D), f32),
            jax.ShapeDtypeStruct((256, D), f32),
        ],
        in_specs=[hbm] * 10,
        out_specs=[vmem] * 4,
        scratch_shapes=[
            pltpu.VMEM((3, ROWS + 16, D), bf16),
            pltpu.VMEM((RIM, D), bf16),
            pltpu.VMEM((1, ROWS), jnp.int32),
            pltpu.VMEM((1, 4), jnp.int32),
            pltpu.VMEM((2, D, 3 * D), bf16),
            pltpu.VMEM((2, D, D), bf16),
            pltpu.VMEM((2, D, 2 * FFH), bf16),
            pltpu.VMEM((2, FFH, D), bf16),
            pltpu.VMEM((D, TOKC), bf16),
            pltpu.VMEM((TOKC, 2 * D), bf16),
            pltpu.VMEM((2, 2, D), bf16),
            pltpu.VMEM((NX, 2, D), bf16),
            pltpu.VMEM((128, 2, D), bf16),
            dma((10,)), dma((3,)), dma((3,)), dma, dma, dma, dma, flag, flag,
        ],
        compiler_params=pltpu.CompilerParams(
            collective_id=1, has_side_effects=True, vmem_limit_bytes=32 * 1024 * 1024
        ),
        name="atoms_tokens",
    )(
        *[
            pltpu.with_memory_space_constraint(a, pltpu.HBM)
            for a in (
                atom_feats, atom_token.reshape(1, ROWS), key_offset.reshape(1, 4),
                w_qkv, w_out, w_up, w_down, w_tok, w_row, w_col,
            )
        ]
    )
    pair_out, atom_out, single = pl.pallas_call(
        finish,
        out_shape=[
            jax.ShapeDtypeStruct(pair_in.shape, bf16),
            jax.ShapeDtypeStruct((ROWS, D), bf16),
            jax.ShapeDtypeStruct((2, TOKC), bf16),
        ],
        in_specs=[vmem] * 5,
        out_specs=[hbm] * 3,
        scratch_shapes=[pltpu.VMEM(pair_in.shape, bf16), dma((10,))],
        compiler_params=pltpu.CompilerParams(vmem_limit_bytes=16 * 1024 * 1024),
        name="pair_add",
    )(pair_in, row_vecs, col_vecs, atoms, means)
    return (atom_out, single, pair_out)


def solution(mesh):
    return jax.shard_map(
        on_device,
        mesh=mesh,
        in_specs=(
            P(("wide", "col"), None),
            P(("wide", "col")),
            P(("wide", "col")),
            P("wide", "col", None),
            P(), P(), P(), P(), P(), P(), P(),
        ),
        out_specs=(P(("wide", "col"), None), P(("wide", "col"), None), P("wide", "col", None)),
        check_vma=False,
    )
```

time: 51.1 us -> 33.2 us (0.65)
  the two profiles are of different devices: /device:TPU:2 before, /device:TPU:1 now
where the time goes in v2:
time: 33.2 us; the launch traced here: 33.1 us
  Pallas kernels  32.4 us (98%)
  between operations  0.66 us (2%)
    pallas_call x1, Pallas kernels, on_device(): pl.pallas_call(functools.partial(kernel, 512 * ROWS), out_shape=[jax.Shap...  31.5 us
    pallas_call x1, Pallas kernels, on_device(): pl.pallas_call(finish, out_shape=[jax.ShapeDtypeStruct(pair_in.shape, bf1...  0.89 us

profile of v2, /device:TPU:1, one launch (start us, length us, event | category | flops | bytes accessed | tf_op | source)
XLA Modules:
  0.0 33.1 jit_solution(8555720993499414243)
XLA Ops:
  0.6 0.0 copy-start
  0.6 31.5 %atoms_tokens.1 = (bf16[128,128]{1,0:T(8,128)(2,1)S(1)}, bf16[2,384]{1,0:T(2,128)(2,1)S(1)}, f32[8,128]{1,0:T(8,128)S(1)}, f32[256,128]{1,0:T(8,128)S(1)}) custom-call(bf16[128,128]{1,0:T(8,128)(2,1)} %feats.1, s32[1,128]{1,0:T(1,128)} %bitcast.2, s32[1,4]{1,0:T(1,128)} %bitcast.3, bf16[2,128,384]{2,1,0:T(8,128)(2,1)} %w_qkv.1, bf16[2,128,128]{2,1,0:T(8,128)(2,1)} %w_out.1, ...), custom_call_target="tpu_custom_call" | custom-call | tf_op jit(solution)/shard_map/atoms_tokens/pallas_call | solution.py:297
  32.2 0.0 copy-done
  32.2 0.9 %pair_add.1 = (bf16[8,256,128]{2,1,0:T(8,128)(2,1)}, bf16[128,128]{1,0:T(8,128)(2,1)}, bf16[2,384]{1,0:T(2,128)(2,1)}) custom-call(bf16[8,256,128]{2,1,0:T(8,128)(2,1)S(1)} %copy-done, f32[8,128]{1,0:T(8,128)S(1)} %get-tuple-element.10.rows, f32[256,128]{1,0:T(8,128)S(1)} %get-tuple-element.11.cols, bf16[128,128]{1,0:T(8,128)(2,1)S(1)} %get-tuple-element.12.atoms, ...), custom_call_target="tpu_custom_call" | custom-call | tf_op jit(solution)/shard_map/pair_add/pallas_call | solution.py:336
Async XLA Ops:
  0.6 31.6 %copy-start = (bf16[8,256,128]{2,1,0:T(8,128)(2,1)S(1)}, bf16[8,256,128]{2,1,0:T(8,128)(2,1)}, u32[]{:S(2)}) copy-start(bf16[8,256,128]{2,1,0:T(8,128)(2,1)} %pair.1) | copy-start | bytes 1572868

commit v3 on v2

--- a/solution.py
+++ b/solution.py
@@ -125,38 +125,19 @@
 SPANS2 = [(64, 128), (192, 64)]
 
 
-def transform(pieces, own_proj, metas, base, n_atoms, wq, wo, wu, wd):
-    left, own, right, far = pieces
-    biases = biases_of(metas, base, n_atoms)
-    rim = project(jnp.concatenate([left, right, far], axis=0), wq[0])
-    proj = jnp.concatenate([rim[:ROWS], own_proj, rim[ROWS:]], axis=0)
-    state = jnp.concatenate([left, own, right, far], axis=0)
-    bias1 = [rows_of(biases[0], 192), rows_of(biases[1], 256), rows_of(biases[2], 256)]
-    state = block(state, proj, SPANS1, bias1, wo[0], wu[0], wd[0])
-    bias2 = [bias1[1], rows_of(biases[2][:2], 192)]
-    proj = project(state, wq[1])
-    return block(state, proj, SPANS2, bias2, wo[1], wu[1], wd[1])
-
-
-def peers():
-    every = [(dy, dz, dc) for dy in range(NY) for dz in range(-7, 9) for dc in range(2)]
-    return sorted(every, key=lambda o: (-(min(o[0], NY - o[0]) + abs(o[1])), -o[2]))
-
-
-def kernel(
-    n_atoms,
+def tell(sem, dev):
+    pl.semaphore_signal(sem, inc=1, device_id=dev, device_id_type=MESH)
+
+
+def halo_kernel(
     feats, tok, koff, w_qkv, w_out, w_up, w_down, w_tok, w_row, w_col,
-    atom_out, single, rows_out, cols_out,
-    halo, far, toks, offs, wq, wo, wu, wd, wt, wp, mine, rowbuf, colbuf,
-    wsem, hsend, hrecv, rsend, rrecv, csend, crecv, around, beyond,
+    atoms, metas, wq, wo, wu, wd, wt, wp,
+    halo, far, toks, offs, wsem, hsend, hrecv,
 ):
-    wide, x = lax.axis_index("wide"), lax.axis_index("col")
-    core = lax.rem(wide, 2)
-    z = lax.rem(wide // 2, NZ)
-    y = wide // (2 * NZ)
-    me = wide * NX + x
-    home = x == y
-
+    me = lax.axis_index("wide") * NX + lax.axis_index("col")
+    barrier = pltpu.get_barrier_semaphore()
+    for step in (-1, 1):
+        tell(barrier, along(step))
     loads = []
     for n, (src, dst) in enumerate(
         [(feats, halo.at[1, pl.ds(0, ROWS)]), (tok, toks), (koff, offs),
@@ -166,26 +147,6 @@
         loads.append(pltpu.make_async_copy(src, dst, wsem.at[n]))
         loads[-1].start()
 
-    def tell(sem, dev):
-        pl.semaphore_signal(sem, inc=1, device_id=dev, device_id_type=MESH)
-
-    def beside(d):
-        return device(y, lax.rem(z + d + NZ, NZ), core, x)
-
-    barrier = pltpu.get_barrier_semaphore()
-    for step in (-1, 1, 2):
-        tell(barrier, along(step))
-    for dy in range(NY):
-        for dx in range(NX):
-            for dc in range(2):
-                if dy or dx or dc:
-                    tell(
-                        barrier,
-                        device(lax.rem(y + dy, NY), z, lax.rem(core + dc, 2), lax.rem(x + dx, NX)),
-                    )
-    for d in NEAR:
-        tell(barrier, beside(d))
-
     for load in loads[:3]:
         load.wait()
     row = lax.broadcasted_iota(jnp.int32, (16, D), 0)
@@ -195,64 +156,121 @@
     )
     meta = jnp.where(row == 0, tok_rel, jnp.where(row == 1, off4, 0.0))
     halo[1, pl.ds(ROWS, 16)] = meta.astype(bf16)
-    pl.semaphore_wait(barrier, 3 + 31 + len(NEAR))
-
-    sends = [
-        pltpu.make_async_remote_copy(
-            halo.at[1], halo.at[0], hsend.at[0], hrecv.at[0], along(1), MESH
-        ),
-        pltpu.make_async_remote_copy(
-            halo.at[1], halo.at[2], hsend.at[1], hrecv.at[1], along(-1), MESH
-        ),
-        pltpu.make_async_remote_copy(
-            halo.at[1, pl.ds(0, RIM)], far, hsend.at[2], hrecv.at[2], along(-2), MESH
-        ),
-    ]
-    for s in sends:
-        s.start()
-
+    pl.semaphore_wait(barrier, 2)
+
+    left = pltpu.make_async_remote_copy(
+        halo.at[1], halo.at[2], hsend.at[1], hrecv.at[1], along(-1), MESH
+    )
+    right = pltpu.make_async_remote_copy(
+        halo.at[1], halo.at[0], hsend.at[0], hrecv.at[0], along(1), MESH
+    )
+    left.start()
+    right.start()
+    left.wait_recv()
+    pass_on = pltpu.make_async_remote_copy(
+        halo.at[2, pl.ds(0, RIM)], far, hsend.at[2], hrecv.at[2], along(-1), MESH
+    )
+    pass_on.start()
+    right.wait_recv()
+    for s in range(3):
+        atoms[pl.ds(s * ROWS, ROWS), :] = halo[s, pl.ds(0, ROWS)]
+        metas[pl.ds(s * 16, 16), :] = halo[s, pl.ds(ROWS, 16)]
+    for load in loads[3:]:
+        load.wait()
+    pass_on.wait_recv()
+    atoms[pl.ds(3 * ROWS, RIM), :] = far[...]
+    for s in (left, right, pass_on):
+        s.wait_send()
+
+
+def kernel(
+    n_atoms,
+    atoms_in, metas_in, wq, wo, wu, wd, wt, wp,
+    atom_out, single, rows_out, cols_out,
+    mine, rowbuf, colbuf,
+    rsend, rrecv, csend, crecv, around, beyond,
+):
+    wide, x = lax.axis_index("wide"), lax.axis_index("col")
+    core = lax.rem(wide, 2)
+    z = lax.rem(wide // 2, NZ)
+    y = wide // (2 * NZ)
+    me = wide * NX + x
+    home = x == y
+    side = (z > NZ // 2).astype(jnp.int32)
+    sign = 2 * side - 1
+    edge = (z < 4) | (z >= NZ - 4)
+
+    def beside(d):
+        return device(y, lax.rem(z + d + NZ, NZ), core, x)
+
+    barrier = pltpu.get_barrier_semaphore()
     for d in NEAR:
-        tell(around, beside(d))
-    loads[3].wait()
-    own = halo[1, pl.ds(0, ROWS)].astype(f32)
-    own_proj = project(own, wq[0])
-    for load in loads[4:]:
-        load.wait()
-    for s in sends:
-        s.wait_recv()
-    pl.semaphore_wait(around, len(NEAR))
-    for d in (4, -4):
-        tell(beyond, beside(d))
-
-    metas = [halo[s, pl.ds(ROWS, 16)].astype(f32) for s in range(3)]
-    pieces = [halo[0, pl.ds(0, ROWS)].astype(f32), own]
-    pieces += [halo[2, pl.ds(0, ROWS)].astype(f32), far[...].astype(f32)]
+        tell(barrier, beside(d))
+    for xs in range(NX):
+        for c in range(2):
+            pl.when(jnp.logical_not(home & (core == c) & (xs == x)))(
+                functools.partial(tell, barrier, device(x, z, c, xs))
+            )
+    for d in range(1, NX):
+        tell(barrier, (wide, lax.rem(x + d, NX)))
+
+    atoms_f = atoms_in[...].astype(f32)
+    metas = [metas_in[pl.ds(16 * s, 16), :].astype(f32) for s in range(3)]
     match, counts = matches(metas[1], metas[2])
-    state = transform(pieces, own_proj, metas, me * ROWS, n_atoms, wq, wo, wu, wd)
+    biases = biases_of(metas, me * ROWS, n_atoms)
+    bias1 = [rows_of(biases[0], 192), rows_of(biases[1], 256), rows_of(biases[2], 256)]
+    state = block(atoms_f, project(atoms_f, wq[0]), SPANS1, bias1, wo[0], wu[0], wd[0])
+
+    pl.semaphore_wait(barrier, 8 + 3 + len(NEAR) - home.astype(jnp.int32))
+    for d in NEAR:
+        tell(around.at[0 if d > 0 else 1], beside(d))
+
+    bias2 = [bias1[1], rows_of(biases[2][:2], 192)]
+    state = block(state, project(state, wq[1]), SPANS2, bias2, wo[1], wu[1], wd[1])
     atoms = state.astype(bf16)
     means, proj = tokens(atoms, match, counts, wt[...], wp[...])
     mine[0] = proj[0:2, :D]
     mine[1] = proj[0:2, D:]
-    pl.semaphore_wait(beyond, 2)
-
-    def send_column(dy, dz, dc):
-        to = device(
-            lax.rem(y + dy, NY), lax.rem(z + dz + NZ, NZ), lax.rem(core + dc, 2), y
-        )
-        pltpu.make_async_remote_copy(
-            mine.at[1], colbuf.at[wide % 32 * NX + x], csend, crecv, to, MESH
-        ).start()
-
-    for dy, dz, dc in peers()[:-1]:
-        send_column(dy, dz, dc)
-    pl.when(jnp.logical_not(home))(functools.partial(send_column, 0, 0, 0))
-    pl.when(home)(
-        pltpu.make_async_copy(mine.at[1], colbuf.at[wide % 32 * NX + x], crecv).start
-    )
+
+    def pass_on(which, direction):
+        pl.semaphore_wait(around.at[which], 4)
+        tell(beyond.at[which], beside(-4 * direction))
+
+    slot = lax.rem(wide, 32) * NX + x
+
+    def send_columns(zd):
+        for dy in (2, 1, 3, 0):
+            for dc in (1, 0):
+                to = device(lax.rem(y + dy, NY), zd, lax.rem(core + dc, 2), y)
+                pltpu.make_async_remote_copy(
+                    mine.at[1], colbuf.at[slot], csend, crecv, to, MESH
+                ).start()
+
+    pass_on(side, sign)
+    pl.when(edge)(functools.partial(pass_on, 1 - side, -sign))
+    pl.semaphore_wait(beyond.at[side], 1)
+    for d in range(8, 0, -1):
+        send_columns(lax.rem(z + sign * d + NZ, NZ))
+    for dy in (2, 1, 3, 0):
+        for dc in (1, 0):
+            to = device(lax.rem(y + dy, NY), z, lax.rem(core + dc, 2), y)
+            copy = pltpu.make_async_remote_copy(
+                mine.at[1], colbuf.at[slot], csend, crecv, to, MESH
+            )
+            if dy or dc:
+                copy.start()
+            else:
+                pl.when(jnp.logical_not(home))(copy.start)
+    pl.when(home)(pltpu.make_async_copy(mine.at[1], colbuf.at[slot], crecv).start)
     for d in range(1, NX):
         pltpu.make_async_remote_copy(
             mine.at[0], rowbuf.at[x], rsend, rrecv, (wide, lax.rem(x + d, NX)), MESH
         ).start()
+    pl.when(jnp.logical_not(edge))(functools.partial(pass_on, 1 - side, -sign))
+    pl.semaphore_wait(beyond.at[1 - side], 1)
+    for d in range(7, 0, -1):
+        send_columns(lax.rem(z - sign * d + NZ, NZ))
+
     rowbuf[pl.ds(x, 1)] = proj[0:2, :D].reshape(1, 2, D)
     atom_out[...] = atoms[:ROWS]
     single[...] = means[0:2]
@@ -261,8 +279,6 @@
     pltpu.make_async_copy(three, three, rrecv).wait()
     for s in range(NX):
         rows_out[pl.ds(2 * s, 2), :] = rowbuf[s].astype(f32)
-    for s in sends:
-        s.wait_send()
     pltpu.make_async_copy(three, three, rsend).wait()
     less = colbuf.at[pl.ds(0, 127)]
     pl.when(home)(pltpu.make_async_copy(less, less, csend).wait)
@@ -293,37 +309,32 @@
 ):
     vmem = pl.BlockSpec(memory_space=pltpu.VMEM)
     hbm = pl.BlockSpec(memory_space=pltpu.HBM)
-    dma, flag = pltpu.SemaphoreType.DMA, pltpu.SemaphoreType.REGULAR
-    atoms, means, row_vecs, col_vecs = pl.pallas_call(
-        functools.partial(kernel, 512 * ROWS),
+    dma = pltpu.SemaphoreType.DMA
+    near = pl.pallas_call(
+        halo_kernel,
         out_shape=[
-            jax.ShapeDtypeStruct((ROWS, D), bf16),
-            jax.ShapeDtypeStruct((2, TOKC), bf16),
-            jax.ShapeDtypeStruct((8, D), f32),
-            jax.ShapeDtypeStruct((256, D), f32),
+            jax.ShapeDtypeStruct((3 * ROWS + RIM, D), bf16),
+            jax.ShapeDtypeStruct((48, D), bf16),
+            jax.ShapeDtypeStruct((2, D, 3 * D), bf16),
+            jax.ShapeDtypeStruct((2, D, D), bf16),
+            jax.ShapeDtypeStruct((2, D, 2 * FFH), bf16),
+            jax.ShapeDtypeStruct((2, FFH, D), bf16),
+            jax.ShapeDtypeStruct((D, TOKC), bf16),
+            jax.ShapeDtypeStruct((TOKC, 2 * D), bf16),
         ],
         in_specs=[hbm] * 10,
-        out_specs=[vmem] * 4,
+        out_specs=[vmem] * 8,
         scratch_shapes=[
             pltpu.VMEM((3, ROWS + 16, D), bf16),
             pltpu.VMEM((RIM, D), bf16),
             pltpu.VMEM((1, ROWS), jnp.int32),
             pltpu.VMEM((1, 4), jnp.int32),
-            pltpu.VMEM((2, D, 3 * D), bf16),
-            pltpu.VMEM((2, D, D), bf16),
-            pltpu.VMEM((2, D, 2 * FFH), bf16),
-            pltpu.VMEM((2, FFH, D), bf16),
-            pltpu.VMEM((D, TOKC), bf16),
-            pltpu.VMEM((TOKC, 2 * D), bf16),
-            pltpu.VMEM((2, 2, D), bf16),
-            pltpu.VMEM((NX, 2, D), bf16),
-            pltpu.VMEM((128, 2, D), bf16),
-            dma((10,)), dma((3,)), dma((3,)), dma, dma, dma, dma, flag, flag,
+            dma((10,)), dma((3,)), dma((3,)),
         ],
         compiler_params=pltpu.CompilerParams(
-            collective_id=1, has_side_effects=True, vmem_limit_bytes=32 * 1024 * 1024
+            collective_id=1, has_side_effects=True, vmem_limit_bytes=16 * 1024 * 1024
         ),
-        name="atoms_tokens",
+        name="halo",
     )(
         *[
             pltpu.with_memory_space_constraint(a, pltpu.HBM)
@@ -333,6 +344,27 @@
             )
         ]
     )
+    atoms, means, row_vecs, col_vecs = pl.pallas_call(
+        functools.partial(kernel, 512 * ROWS),
+        out_shape=[
+            jax.ShapeDtypeStruct((ROWS, D), bf16),
+            jax.ShapeDtypeStruct((2, TOKC), bf16),
+            jax.ShapeDtypeStruct((8, D), f32),
+            jax.ShapeDtypeStruct((256, D), f32),
+        ],
+        in_specs=[vmem] * 8,
+        out_specs=[vmem] * 4,
+        scratch_shapes=[
+            pltpu.VMEM((2, 2, D), bf16),
+            pltpu.VMEM((NX, 2, D), bf16),
+            pltpu.VMEM((128, 2, D), bf16),
+            dma, dma, dma, dma, pltpu.SemaphoreType.REGULAR((2,)), pltpu.SemaphoreType.REGULAR((2,)),
+        ],
+        compiler_params=pltpu.CompilerParams(
+            collective_id=2, has_side_effects=True, vmem_limit_bytes=32 * 1024 * 1024
+        ),
+        name="atoms_tokens",
+    )(*near)
     pair_out, atom_out, single = pl.pallas_call(
         finish,
         out_shape=[

time: 33.2 us -> 40 us (1.20)
  the two profiles are of different devices: /device:TPU:1 before, /device:TPU:4 now
where the time goes in v3:
time: 40 us; the launch traced here: 39.8 us
  Pallas kernels  39.2 us (98%)
  between operations  0.67 us (2%)
    pallas_call x1, Pallas kernels, on_device(): pl.pallas_call(functools.partial(kernel, 512 * ROWS), out_shape=[jax.Shap...  29 us
    pallas_call x1, Pallas kernels, on_device(): pl.pallas_call(halo_kernel, out_shape=[jax.ShapeDtypeStruct((3 * ROWS + R...  9.28 us
    pallas_call x1, Pallas kernels, on_device(): pl.pallas_call(finish, out_shape=[jax.ShapeDtypeStruct(pair_in.shape, bf1...  0.89 us

profile of v3, /device:TPU:4, one launch (start us, length us, event | category | flops | bytes accessed | tf_op | source)
XLA Modules:
  0.0 39.8 jit_solution(10428170441736357572)
XLA Ops:
  0.6 9.3 %halo.1 = (bf16[448,128]{1,0:T(8,128)(2,1)S(1)}, bf16[48,128]{1,0:T(8,128)(2,1)S(1)}, bf16[2,128,384]{2,1,0:T(8,128)(2,1)S(1)}, bf16[2,128,128]{2,1,0:T(8,128)(2...) custom-call(bf16[128,128]{1,0:T(8,128)(2,1)} %feats.1, ...), custom_call_target="tpu_custom_call" | custom-call | tf_op jit(solution)/shard_map/halo/pallas_call | solution.py:313
  9.9 0.0 copy-start
  9.9 29.0 %atoms_tokens.1 = (bf16[128,128]{1,0:T(8,128)(2,1)S(1)}, bf16[2,384]{1,0:T(2,128)(2,1)S(1)}, f32[8,128]{1,0:T(8,128)S(1)}, f32[256,128]{1,0:T(8,128)S(1)}) custom-call(bf16[448,128]{1,0:T(8,128)(2,1)S(1)} %get-tuple-element.18.atoms_in, bf16[48,128]{1,0:T(8,128)(2,1)S(1)} %get-tuple-element.19.metas_in, bf16[2,128,384]{2,1,0:T(8,128)(2,1)S(1)} %get-tuple-element.20.wq, ...), custom_call_target="tpu_custom_call" | custom-call | tf_op jit(solution)/shard_map/atoms_tokens/pallas_call | solution.py:347
  39.0 0.0 copy-done
  39.0 0.9 %pair_add.1 = (bf16[8,256,128]{2,1,0:T(8,128)(2,1)}, bf16[128,128]{1,0:T(8,128)(2,1)}, bf16[2,384]{1,0:T(2,128)(2,1)}) custom-call(bf16[8,256,128]{2,1,0:T(8,128)(2,1)S(1)} %copy-done, f32[8,128]{1,0:T(8,128)S(1)} %get-tuple-element.26.rows, f32[256,128]{1,0:T(8,128)S(1)} %get-tuple-element.27.cols, bf16[128,128]{1,0:T(8,128)(2,1)S(1)} %get-tuple-element.28.atoms, ...), custom_call_target="tpu_custom_call" | custom-call | tf_op jit(solution)/shard_map/pair_add/pallas_call | solution.py:368
Async XLA Ops:
  9.9 29.0 %copy-start = (bf16[8,256,128]{2,1,0:T(8,128)(2,1)S(1)}, bf16[8,256,128]{2,1,0:T(8,128)(2,1)}, u32[]{:S(2)}) copy-start(bf16[8,256,128]{2,1,0:T(8,128)(2,1)} %pair.1) | copy-start | bytes 1572868

commit v4 on v2

--- a/solution.py
+++ b/solution.py
@@ -157,6 +157,25 @@
     me = wide * NX + x
     home = x == y
 
+    def tell(sem, dev):
+        pl.semaphore_signal(sem, inc=1, device_id=dev, device_id_type=MESH)
+
+    def beside(d):
+        return device(y, lax.rem(z + d + NZ, NZ), core, x)
+
+    barrier = pltpu.get_barrier_semaphore()
+    for step in (-1, 1, 2):
+        tell(barrier, along(step))
+    for d in NEAR:
+        tell(barrier, beside(d))
+    for xs in range(NX):
+        for c in range(2):
+            pl.when(jnp.logical_not(home & (core == c) & (xs == x)))(
+                functools.partial(tell, barrier, device(x, z, c, xs))
+            )
+    for d in range(1, NX):
+        tell(barrier, (wide, lax.rem(x + d, NX)))
+
     loads = []
     for n, (src, dst) in enumerate(
         [(feats, halo.at[1, pl.ds(0, ROWS)]), (tok, toks), (koff, offs),
@@ -166,26 +185,6 @@
         loads.append(pltpu.make_async_copy(src, dst, wsem.at[n]))
         loads[-1].start()
 
-    def tell(sem, dev):
-        pl.semaphore_signal(sem, inc=1, device_id=dev, device_id_type=MESH)
-
-    def beside(d):
-        return device(y, lax.rem(z + d + NZ, NZ), core, x)
-
-    barrier = pltpu.get_barrier_semaphore()
-    for step in (-1, 1, 2):
-        tell(barrier, along(step))
-    for dy in range(NY):
-        for dx in range(NX):
-            for dc in range(2):
-                if dy or dx or dc:
-                    tell(
-                        barrier,
-                        device(lax.rem(y + dy, NY), z, lax.rem(core + dc, 2), lax.rem(x + dx, NX)),
-                    )
-    for d in NEAR:
-        tell(barrier, beside(d))
-
     for load in loads[:3]:
         load.wait()
     row = lax.broadcasted_iota(jnp.int32, (16, D), 0)
@@ -195,7 +194,7 @@
     )
     meta = jnp.where(row == 0, tok_rel, jnp.where(row == 1, off4, 0.0))
     halo[1, pl.ds(ROWS, 16)] = meta.astype(bf16)
-    pl.semaphore_wait(barrier, 3 + 31 + len(NEAR))
+    pl.semaphore_wait(barrier, 3 + 8 + 3 + len(NEAR) - home.astype(jnp.int32))
 
     sends = [
         pltpu.make_async_remote_copy(
@@ -235,17 +234,19 @@
     mine[1] = proj[0:2, D:]
     pl.semaphore_wait(beyond, 2)
 
-    def send_column(dy, dz, dc):
-        to = device(
-            lax.rem(y + dy, NY), lax.rem(z + dz + NZ, NZ), lax.rem(core + dc, 2), y
-        )
+    def send_column(to):
         pltpu.make_async_remote_copy(
             mine.at[1], colbuf.at[wide % 32 * NX + x], csend, crecv, to, MESH
         ).start()
 
-    for dy, dz, dc in peers()[:-1]:
-        send_column(dy, dz, dc)
-    pl.when(jnp.logical_not(home))(functools.partial(send_column, 0, 0, 0))
+    for zd in range(NZ):
+        for dy in (2, 1, 3, 0):
+            for dc in (1, 0):
+                to = device(lax.rem(y + dy, NY), zd, lax.rem(core + dc, 2), y)
+                if dy or dc:
+                    send_column(to)
+                else:
+                    pl.when(jnp.logical_not(home & (z == zd)))(functools.partial(send_column, to))
     pl.when(home)(
         pltpu.make_async_copy(mine.at[1], colbuf.at[wide % 32 * NX + x], crecv).start
     )
@@ -261,15 +262,15 @@
     pltpu.make_async_copy(three, three, rrecv).wait()
     for s in range(NX):
         rows_out[pl.ds(2 * s, 2), :] = rowbuf[s].astype(f32)
+    pltpu.make_async_copy(colbuf, colbuf, crecv).wait()
+    for s in range(128):
+        cols_out[pl.ds(2 * s, 2), :] = colbuf[s].astype(f32)
     for s in sends:
         s.wait_send()
     pltpu.make_async_copy(three, three, rsend).wait()
     less = colbuf.at[pl.ds(0, 127)]
     pl.when(home)(pltpu.make_async_copy(less, less, csend).wait)
     pl.when(jnp.logical_not(home))(pltpu.make_async_copy(colbuf, colbuf, csend).wait)
-    pltpu.make_async_copy(colbuf, colbuf, crecv).wait()
-    for s in range(128):
-        cols_out[pl.ds(2 * s, 2), :] = colbuf[s].astype(f32)
 
 
 def finish(pair, rows, cols, atoms, means, pair_out, atom_out, single, sums, sem):

time: 33.2 us -> 32 us (0.964)
  the two profiles are of different devices: /device:TPU:1 before, /device:TPU:4 now
where the time goes in v4:
time: 32 us; the launch traced here: 31.9 us
  Pallas kernels  31.3 us (98%)
  between operations  0.66 us (2%)
    pallas_call x1, Pallas kernels, on_device(): pl.pallas_call(functools.partial(kernel, 512 * ROWS), out_shape=[jax.Shap...  30.4 us
    pallas_call x1, Pallas kernels, on_device(): pl.pallas_call(finish, out_shape=[jax.ShapeDtypeStruct(pair_in.shape, bf1...  0.89 us

profile of v4, /device:TPU:4, one launch (start us, length us, event | category | flops | bytes accessed | tf_op | source)
XLA Modules:
  0.0 31.9 jit_solution(5447197529273033414)
XLA Ops:
  0.6 0.0 copy-start
  0.6 30.4 %atoms_tokens.1 = (bf16[128,128]{1,0:T(8,128)(2,1)S(1)}, bf16[2,384]{1,0:T(2,128)(2,1)S(1)}, f32[8,128]{1,0:T(8,128)S(1)}, f32[256,128]{1,0:T(8,128)S(1)}) custom-call(bf16[128,128]{1,0:T(8,128)(2,1)} %feats.1, s32[1,128]{1,0:T(1,128)} %bitcast.2, s32[1,4]{1,0:T(1,128)} %bitcast.3, bf16[2,128,384]{2,1,0:T(8,128)(2,1)} %w_qkv.1, bf16[2,128,128]{2,1,0:T(8,128)(2,1)} %w_out.1, ...), custom_call_target="tpu_custom_call" | custom-call | tf_op jit(solution)/shard_map/atoms_tokens/pallas_call | solution.py:298
  31.0 0.0 copy-done
  31.0 0.9 %pair_add.1 = (bf16[8,256,128]{2,1,0:T(8,128)(2,1)}, bf16[128,128]{1,0:T(8,128)(2,1)}, bf16[2,384]{1,0:T(2,128)(2,1)}) custom-call(bf16[8,256,128]{2,1,0:T(8,128)(2,1)S(1)} %copy-done, f32[8,128]{1,0:T(8,128)S(1)} %get-tuple-element.10.rows, f32[256,128]{1,0:T(8,128)S(1)} %get-tuple-element.11.cols, bf16[128,128]{1,0:T(8,128)(2,1)S(1)} %get-tuple-element.12.atoms, ...), custom_call_target="tpu_custom_call" | custom-call | tf_op jit(solution)/shard_map/pair_add/pallas_call | solution.py:337
Async XLA Ops:
  0.6 30.4 %copy-start = (bf16[8,256,128]{2,1,0:T(8,128)(2,1)S(1)}, bf16[8,256,128]{2,1,0:T(8,128)(2,1)}, u32[]{:S(2)}) copy-start(bf16[8,256,128]{2,1,0:T(8,128)(2,1)} %pair.1) | copy-start | bytes 1572868

commit v5 on v4

--- a/solution.py
+++ b/solution.py
@@ -17,7 +17,7 @@
 RIM = 64
 ROWS = 128
 NY, NZ, NX = 4, 16, 4
-NEAR = (4, -4, 3, -3, 2, -2, 1, -1)
+NEAR = (2, -2, 1, -1)
 SCORE = 1.4426950408889634 / HEAD**0.5
 NEG = -1e30
 MESH = pl.DeviceIdType.MESH
@@ -37,9 +37,10 @@
     return jnp.dot(a, b, preferred_element_type=f32)
 
 
-def norm(v):
+def normed_dot(v, w):
     c = v - jnp.mean(v, axis=-1, keepdims=True)
-    return (c * lax.rsqrt(jnp.mean(c * c, axis=-1, keepdims=True) + 1e-5)).astype(bf16)
+    scale = lax.rsqrt(jnp.mean(c * c, axis=-1, keepdims=True) + 1e-5)
+    return dot(c.astype(bf16), w) * scale
 
 
 def window_bias(offset, block, base, n_key, n_atoms):
@@ -86,14 +87,14 @@
     first = spans[0][0]
     last = spans[-1][0] + spans[-1][1]
     state = state[first:last] + dot(jnp.concatenate(kept, axis=0), wo)
-    hidden = dot(norm(state), wu)
+    hidden = normed_dot(state, wu)
     gate, up = hidden[:, :FFH], hidden[:, FFH:]
     gated = (0.5 * gate * (1.0 + jnp.tanh(0.5 * gate)) * up).astype(bf16)
     return state + dot(gated, wd)
 
 
 def project(rows, wq):
-    return dot(norm(rows), wq).astype(bf16)
+    return normed_dot(rows, wq).astype(bf16)
 
 
 def tokens(atoms, match, counts, wt, wp):
@@ -125,7 +126,7 @@
 SPANS2 = [(64, 128), (192, 64)]
 
 
-def transform(pieces, own_proj, metas, base, n_atoms, wq, wo, wu, wd):
+def transform(pieces, own_proj, metas, base, n_atoms, wq, wo, wu, wd, between):
     left, own, right, far = pieces
     biases = biases_of(metas, base, n_atoms)
     rim = project(jnp.concatenate([left, right, far], axis=0), wq[0])
@@ -133,6 +134,7 @@
     state = jnp.concatenate([left, own, right, far], axis=0)
     bias1 = [rows_of(biases[0], 192), rows_of(biases[1], 256), rows_of(biases[2], 256)]
     state = block(state, proj, SPANS1, bias1, wo[0], wu[0], wd[0])
+    between()
     bias2 = [bias1[1], rows_of(biases[2][:2], 192)]
     proj = project(state, wq[1])
     return block(state, proj, SPANS2, bias2, wo[1], wu[1], wd[1])
@@ -148,7 +150,7 @@
     feats, tok, koff, w_qkv, w_out, w_up, w_down, w_tok, w_row, w_col,
     atom_out, single, rows_out, cols_out,
     halo, far, toks, offs, wq, wo, wu, wd, wt, wp, mine, rowbuf, colbuf,
-    wsem, hsend, hrecv, rsend, rrecv, csend, crecv, around, beyond,
+    wsem, hsend, hrecv, rsend, rrecv, csend, crecv, around, beyond, rest,
 ):
     wide, x = lax.axis_index("wide"), lax.axis_index("col")
     core = lax.rem(wide, 2)
@@ -217,22 +219,28 @@
     own_proj = project(own, wq[0])
     for load in loads[4:]:
         load.wait()
-    for s in sends:
-        s.wait_recv()
     pl.semaphore_wait(around, len(NEAR))
     for d in (4, -4):
         tell(beyond, beside(d))
+    for s in sends:
+        s.wait_recv()
 
     metas = [halo[s, pl.ds(ROWS, 16)].astype(f32) for s in range(3)]
     pieces = [halo[0, pl.ds(0, ROWS)].astype(f32), own]
     pieces += [halo[2, pl.ds(0, ROWS)].astype(f32), far[...].astype(f32)]
     match, counts = matches(metas[1], metas[2])
-    state = transform(pieces, own_proj, metas, me * ROWS, n_atoms, wq, wo, wu, wd)
+
+    def pass_on():
+        pl.semaphore_wait(beyond, 2)
+        for d in (2, -2):
+            tell(rest, beside(d))
+
+    state = transform(pieces, own_proj, metas, me * ROWS, n_atoms, wq, wo, wu, wd, pass_on)
     atoms = state.astype(bf16)
     means, proj = tokens(atoms, match, counts, wt[...], wp[...])
     mine[0] = proj[0:2, :D]
     mine[1] = proj[0:2, D:]
-    pl.semaphore_wait(beyond, 2)
+    pl.semaphore_wait(rest, 2)
 
     def send_column(to):
         pltpu.make_async_remote_copy(
@@ -319,7 +327,7 @@
             pltpu.VMEM((2, 2, D), bf16),
             pltpu.VMEM((NX, 2, D), bf16),
             pltpu.VMEM((128, 2, D), bf16),
-            dma((10,)), dma((3,)), dma((3,)), dma, dma, dma, dma, flag, flag,
+            dma((10,)), dma((3,)), dma((3,)), dma, dma, dma, dma, flag, flag, flag,
         ],
         compiler_params=pltpu.CompilerParams(
             collective_id=1, has_side_effects=True, vmem_limit_bytes=32 * 1024 * 1024

time: 32 us -> 31.6 us (0.988)
  Pallas kernels: 31.3 us -> 30.8 us
    pallas_call x1, Pallas kernels: 30.4 us -> 29.9 us  [on_device(): pl.pallas_call(functools.partial(kernel, 512 * ROWS), out_shape=[jax.Shap...]
where the time goes in v5:
time: 31.6 us; the launch traced here: 31.4 us
  Pallas kernels  30.8 us (97%)
  between operations  0.66 us (2%)
    pallas_call x1, Pallas kernels, on_device(): pl.pallas_call(functools.partial(kernel, 512 * ROWS), out_shape=[jax.Shap...  29.9 us
    pallas_call x1, Pallas kernels, on_device(): pl.pallas_call(finish, out_shape=[jax.ShapeDtypeStruct(pair_in.shape, bf1...  0.89 us

profile of v5, /device:TPU:4, one launch (start us, length us, event | category | flops | bytes accessed | tf_op | source)
XLA Modules:
  0.0 31.4 jit_solution(16372945055838837879)
XLA Ops:
  0.6 0.0 copy-start
  0.6 29.9 %atoms_tokens.1 = (bf16[128,128]{1,0:T(8,128)(2,1)S(1)}, bf16[2,384]{1,0:T(2,128)(2,1)S(1)}, f32[8,128]{1,0:T(8,128)S(1)}, f32[256,128]{1,0:T(8,128)S(1)}) custom-call(bf16[128,128]{1,0:T(8,128)(2,1)} %feats.1, s32[1,128]{1,0:T(1,128)} %bitcast.2, s32[1,4]{1,0:T(1,128)} %bitcast.3, bf16[2,128,384]{2,1,0:T(8,128)(2,1)} %w_qkv.1, bf16[2,128,128]{2,1,0:T(8,128)(2,1)} %w_out.1, ...), custom_call_target="tpu_custom_call" | custom-call | tf_op jit(solution)/shard_map/atoms_tokens/pallas_call | solution.py:306
  30.6 0.0 copy-done
  30.6 0.9 %pair_add.1 = (bf16[8,256,128]{2,1,0:T(8,128)(2,1)}, bf16[128,128]{1,0:T(8,128)(2,1)}, bf16[2,384]{1,0:T(2,128)(2,1)}) custom-call(bf16[8,256,128]{2,1,0:T(8,128)(2,1)S(1)} %copy-done, f32[8,128]{1,0:T(8,128)S(1)} %get-tuple-element.10.rows, f32[256,128]{1,0:T(8,128)S(1)} %get-tuple-element.11.cols, bf16[128,128]{1,0:T(8,128)(2,1)S(1)} %get-tuple-element.12.atoms, ...), custom_call_target="tpu_custom_call" | custom-call | tf_op jit(solution)/shard_map/pair_add/pallas_call | solution.py:345
Async XLA Ops:
  0.6 29.9 %copy-start = (bf16[8,256,128]{2,1,0:T(8,128)(2,1)S(1)}, bf16[8,256,128]{2,1,0:T(8,128)(2,1)}, u32[]{:S(2)}) copy-start(bf16[8,256,128]{2,1,0:T(8,128)(2,1)} %pair.1) | copy-start | bytes 1572868

commit v6 on v5

--- a/solution.py
+++ b/solution.py
@@ -209,7 +209,7 @@
             halo.at[1, pl.ds(0, RIM)], far, hsend.at[2], hrecv.at[2], along(-2), MESH
         ),
     ]
-    for s in sends:
+    for s in (sends[2], sends[0], sends[1]):
         s.start()
 
     for d in NEAR:
@@ -221,7 +221,7 @@
         load.wait()
     pl.semaphore_wait(around, len(NEAR))
     for d in (4, -4):
-        tell(beyond, beside(d))
+        tell(beyond.at[0 if d > 0 else 1], beside(d))
     for s in sends:
         s.wait_recv()
 
@@ -230,33 +230,51 @@
     pieces += [halo[2, pl.ds(0, ROWS)].astype(f32), far[...].astype(f32)]
     match, counts = matches(metas[1], metas[2])
 
-    def pass_on():
-        pl.semaphore_wait(beyond, 2)
-        for d in (2, -2):
-            tell(rest, beside(d))
-
-    state = transform(pieces, own_proj, metas, me * ROWS, n_atoms, wq, wo, wu, wd, pass_on)
+    near_side = (z > NZ // 2).astype(jnp.int32)
+
+    def pass_on(which):
+        pl.semaphore_wait(beyond.at[which], 1)
+        tell(rest.at[which], beside(2 - 4 * which))
+
+    state = transform(pieces, own_proj, metas, me * ROWS, n_atoms, wq, wo, wu, wd, functools.partial(pass_on, near_side))
     atoms = state.astype(bf16)
     means, proj = tokens(atoms, match, counts, wt[...], wp[...])
     mine[0] = proj[0:2, :D]
     mine[1] = proj[0:2, D:]
-    pl.semaphore_wait(rest, 2)
-
-    def send_column(to):
-        pltpu.make_async_remote_copy(
-            mine.at[1], colbuf.at[wide % 32 * NX + x], csend, crecv, to, MESH
-        ).start()
-
-    for zd in range(NZ):
-        for dy in (2, 1, 3, 0):
-            for dc in (1, 0):
-                to = device(lax.rem(y + dy, NY), zd, lax.rem(core + dc, 2), y)
-                if dy or dc:
-                    send_column(to)
-                else:
-                    pl.when(jnp.logical_not(home & (z == zd)))(functools.partial(send_column, to))
+    slot = lax.rem(wide, 32) * NX + x
+
+    def send_columns(zd, _, part):
+        ahead = lax.rem((z - zd) * (1 - 2 * near_side) + NZ, NZ)
+        beside_me = (ahead <= 2) | (ahead >= NZ - 2)
+        this = (beside_me, (ahead > 2) & (ahead <= 8), (ahead > 8) & (ahead < NZ - 2))[part]
+
+        @pl.when(this)
+        def _():
+            for dy in (2, 1, 3, 0):
+                for dc in (1, 0):
+                    to = device(lax.rem(y + dy, NY), zd, lax.rem(core + dc, 2), y)
+                    copy = pltpu.make_async_remote_copy(
+                        mine.at[1], colbuf.at[slot], csend, crecv, to, MESH
+                    )
+                    if dy or dc:
+                        copy.start()
+                    else:
+                        pl.when(jnp.logical_not(home & (z == zd)))(copy.start)
+
+        return 0
+
+    def send_part(part):
+        lax.fori_loop(0, NZ, functools.partial(send_columns, part=part), 0)
+
+    pass_on(1 - near_side)
+    pl.when(z < 4)(functools.partial(send_part, 0))
+    pl.semaphore_wait(rest.at[near_side], 1)
+    send_part(1)
+    pl.when(z >= 4)(functools.partial(send_part, 0))
+    pl.semaphore_wait(rest.at[1 - near_side], 1)
+    send_part(2)
     pl.when(home)(
-        pltpu.make_async_copy(mine.at[1], colbuf.at[wide % 32 * NX + x], crecv).start
+        pltpu.make_async_copy(mine.at[1], colbuf.at[slot], crecv).start
     )
     for d in range(1, NX):
         pltpu.make_async_remote_copy(
@@ -327,7 +345,7 @@
             pltpu.VMEM((2, 2, D), bf16),
             pltpu.VMEM((NX, 2, D), bf16),
             pltpu.VMEM((128, 2, D), bf16),
-            dma((10,)), dma((3,)), dma((3,)), dma, dma, dma, dma, flag, flag, flag,
+            dma((10,)), dma((3,)), dma((3,)), dma, dma, dma, dma, flag, flag((2,)), flag((2,)),
         ],
         compiler_params=pltpu.CompilerParams(
             collective_id=1, has_side_effects=True, vmem_limit_bytes=32 * 1024 * 1024

time: 31.6 us -> 31.3 us (level)
  no operation moved by 1% of the time
where the time goes in v6:
time: 31.3 us; the launch traced here: 31.2 us
  Pallas kernels  30.5 us (97%)
  between operations  0.66 us (2%)
    pallas_call x1, Pallas kernels, on_device(): pl.pallas_call(functools.partial(kernel, 512 * ROWS), out_shape=[jax.Shap...  29.7 us
    pallas_call x1, Pallas kernels, on_device(): pl.pallas_call(finish, out_shape=[jax.ShapeDtypeStruct(pair_in.shape, bf1...  0.89 us

profile of v6, /device:TPU:4, one launch (start us, length us, event | category | flops | bytes accessed | tf_op | source)
XLA Modules:
  0.0 31.2 jit_solution(7021228026120885809)
XLA Ops:
  0.6 0.0 copy-start
  0.6 29.7 %atoms_tokens.1 = (bf16[128,128]{1,0:T(8,128)(2,1)S(1)}, bf16[2,384]{1,0:T(2,128)(2,1)S(1)}, f32[8,128]{1,0:T(8,128)S(1)}, f32[256,128]{1,0:T(8,128)S(1)}) custom-call(bf16[128,128]{1,0:T(8,128)(2,1)} %feats.1, s32[1,128]{1,0:T(1,128)} %bitcast.2, s32[1,4]{1,0:T(1,128)} %bitcast.3, bf16[2,128,384]{2,1,0:T(8,128)(2,1)} %w_qkv.1, bf16[2,128,128]{2,1,0:T(8,128)(2,1)} %w_out.1, ...), custom_call_target="tpu_custom_call" | custom-call | tf_op jit(solution)/shard_map/atoms_tokens/pallas_call | solution.py:324
  30.3 0.0 copy-done
  30.3 0.9 %pair_add.1 = (bf16[8,256,128]{2,1,0:T(8,128)(2,1)}, bf16[128,128]{1,0:T(8,128)(2,1)}, bf16[2,384]{1,0:T(2,128)(2,1)}) custom-call(bf16[8,256,128]{2,1,0:T(8,128)(2,1)S(1)} %copy-done, f32[8,128]{1,0:T(8,128)S(1)} %get-tuple-element.10.rows, f32[256,128]{1,0:T(8,128)S(1)} %get-tuple-element.11.cols, bf16[128,128]{1,0:T(8,128)(2,1)S(1)} %get-tuple-element.12.atoms, ...), custom_call_target="tpu_custom_call" | custom-call | tf_op jit(solution)/shard_map/pair_add/pallas_call | solution.py:363
Async XLA Ops:
  0.6 29.7 %copy-start = (bf16[8,256,128]{2,1,0:T(8,128)(2,1)S(1)}, bf16[8,256,128]{2,1,0:T(8,128)(2,1)}, u32[]{:S(2)}) copy-start(bf16[8,256,128]{2,1,0:T(8,128)(2,1)} %pair.1) | copy-start | bytes 1572868

commit v7 on v6

--- a/solution.py
+++ b/solution.py
@@ -140,11 +140,6 @@
     return block(state, proj, SPANS2, bias2, wo[1], wu[1], wd[1])
 
 
-def peers():
-    every = [(dy, dz, dc) for dy in range(NY) for dz in range(-7, 9) for dc in range(2)]
-    return sorted(every, key=lambda o: (-(min(o[0], NY - o[0]) + abs(o[1])), -o[2]))
-
-
 def kernel(
     n_atoms,
     feats, tok, koff, w_qkv, w_out, w_up, w_down, w_tok, w_row, w_col,
@@ -236,7 +231,10 @@
         pl.semaphore_wait(beyond.at[which], 1)
         tell(rest.at[which], beside(2 - 4 * which))
 
-    state = transform(pieces, own_proj, metas, me * ROWS, n_atoms, wq, wo, wu, wd, functools.partial(pass_on, near_side))
+    state = transform(
+        pieces, own_proj, metas, me * ROWS, n_atoms, wq, wo, wu, wd,
+        functools.partial(pass_on, near_side),
+    )
     atoms = state.astype(bf16)
     means, proj = tokens(atoms, match, counts, wt[...], wp[...])
     mine[0] = proj[0:2, :D]
@@ -266,10 +264,12 @@
     def send_part(part):
         lax.fori_loop(0, NZ, functools.partial(send_columns, part=part), 0)
 
-    pass_on(1 - near_side)
+    edge = (z < 4) | (z >= NZ - 4)
+    pl.when(edge)(functools.partial(pass_on, 1 - near_side))
     pl.when(z < 4)(functools.partial(send_part, 0))
     pl.semaphore_wait(rest.at[near_side], 1)
     send_part(1)
+    pl.when(jnp.logical_not(edge))(functools.partial(pass_on, 1 - near_side))
     pl.when(z >= 4)(functools.partial(send_part, 0))
     pl.semaphore_wait(rest.at[1 - near_side], 1)
     send_part(2)

time: 31.3 us -> 31.3 us (level)
  no operation moved by 1% of the time
where the time goes in v7:
time: 31.3 us; the launch traced here: 31.2 us
  Pallas kernels  30.5 us (97%)
  between operations  0.66 us (2%)
    pallas_call x1, Pallas kernels, on_device(): pl.pallas_call(functools.partial(kernel, 512 * ROWS), out_shape=[jax.Shap...  29.6 us
    pallas_call x1, Pallas kernels, on_device(): pl.pallas_call(finish, out_shape=[jax.ShapeDtypeStruct(pair_in.shape, bf1...  0.89 us

profile of v7, /device:TPU:4, one launch (start us, length us, event | category | flops | bytes accessed | tf_op | source)
XLA Modules:
  0.0 31.2 jit_solution(1185330971196266346)
XLA Ops:
  0.6 0.0 copy-start
  0.6 29.6 %atoms_tokens.1 = (bf16[128,128]{1,0:T(8,128)(2,1)S(1)}, bf16[2,384]{1,0:T(2,128)(2,1)S(1)}, f32[8,128]{1,0:T(8,128)S(1)}, f32[256,128]{1,0:T(8,128)S(1)}) custom-call(bf16[128,128]{1,0:T(8,128)(2,1)} %feats.1, s32[1,128]{1,0:T(1,128)} %bitcast.2, s32[1,4]{1,0:T(1,128)} %bitcast.3, bf16[2,128,384]{2,1,0:T(8,128)(2,1)} %w_qkv.1, bf16[2,128,128]{2,1,0:T(8,128)(2,1)} %w_out.1, ...), custom_call_target="tpu_custom_call" | custom-call | tf_op jit(solution)/shard_map/atoms_tokens/pallas_call | solution.py:324
  30.3 0.0 copy-done
  30.3 0.9 %pair_add.1 = (bf16[8,256,128]{2,1,0:T(8,128)(2,1)}, bf16[128,128]{1,0:T(8,128)(2,1)}, bf16[2,384]{1,0:T(2,128)(2,1)}) custom-call(bf16[8,256,128]{2,1,0:T(8,128)(2,1)S(1)} %copy-done, f32[8,128]{1,0:T(8,128)S(1)} %get-tuple-element.10.rows, f32[256,128]{1,0:T(8,128)S(1)} %get-tuple-element.11.cols, bf16[128,128]{1,0:T(8,128)(2,1)S(1)} %get-tuple-element.12.atoms, ...), custom_call_target="tpu_custom_call" | custom-call | tf_op jit(solution)/shard_map/pair_add/pallas_call | solution.py:363
Async XLA Ops:
  0.6 29.7 %copy-start = (bf16[8,256,128]{2,1,0:T(8,128)(2,1)S(1)}, bf16[8,256,128]{2,1,0:T(8,128)(2,1)}, u32[]{:S(2)}) copy-start(bf16[8,256,128]{2,1,0:T(8,128)(2,1)} %pair.1) | copy-start | bytes 1572868

commit v8 on v7

--- a/solution.py
+++ b/solution.py
@@ -163,13 +163,13 @@
     barrier = pltpu.get_barrier_semaphore()
     for step in (-1, 1, 2):
         tell(barrier, along(step))
-    for d in NEAR:
-        tell(barrier, beside(d))
     for xs in range(NX):
         for c in range(2):
             pl.when(jnp.logical_not(home & (core == c) & (xs == x)))(
                 functools.partial(tell, barrier, device(x, z, c, xs))
             )
+    for d in NEAR:
+        tell(barrier, beside(d))
     for d in range(1, NX):
         tell(barrier, (wide, lax.rem(x + d, NX)))
 
@@ -221,8 +221,10 @@
         s.wait_recv()
 
     metas = [halo[s, pl.ds(ROWS, 16)].astype(f32) for s in range(3)]
-    pieces = [halo[0, pl.ds(0, ROWS)].astype(f32), own]
-    pieces += [halo[2, pl.ds(0, ROWS)].astype(f32), far[...].astype(f32)]
+    ends = n_atoms // ROWS
+    left = jnp.where(me == 0, 0.0, halo[0, pl.ds(0, ROWS)].astype(f32))
+    right = jnp.where(me == ends - 1, 0.0, halo[2, pl.ds(0, ROWS)].astype(f32))
+    pieces = [left, own, right, jnp.where(me >= ends - 2, 0.0, far[...].astype(f32))]
     match, counts = matches(metas[1], metas[2])
 
     near_side = (z > NZ // 2).astype(jnp.int32)

time: 31.3 us -> 31.4 us (level)
  no operation moved by 1% of the time
where the time goes in v8:
time: 31.4 us; the launch traced here: 31.3 us
  Pallas kernels  30.6 us (97%)
  between operations  0.66 us (2%)
    pallas_call x1, Pallas kernels, on_device(): pl.pallas_call(functools.partial(kernel, 512 * ROWS), out_shape=[jax.Shap...  29.7 us
    pallas_call x1, Pallas kernels, on_device(): pl.pallas_call(finish, out_shape=[jax.ShapeDtypeStruct(pair_in.shape, bf1...  0.89 us

profile of v8, /device:TPU:4, one launch (start us, length us, event | category | flops | bytes accessed | tf_op | source)
XLA Modules:
  0.0 31.3 jit_solution(12542797397325328669)
XLA Ops:
  0.6 0.0 copy-start
  0.6 29.7 %atoms_tokens.1 = (bf16[128,128]{1,0:T(8,128)(2,1)S(1)}, bf16[2,384]{1,0:T(2,128)(2,1)S(1)}, f32[8,128]{1,0:T(8,128)S(1)}, f32[256,128]{1,0:T(8,128)S(1)}) custom-call(bf16[128,128]{1,0:T(8,128)(2,1)} %feats.1, s32[1,128]{1,0:T(1,128)} %bitcast.2, s32[1,4]{1,0:T(1,128)} %bitcast.3, bf16[2,128,384]{2,1,0:T(8,128)(2,1)} %w_qkv.1, bf16[2,128,128]{2,1,0:T(8,128)(2,1)} %w_out.1, ...), custom_call_target="tpu_custom_call" | custom-call | tf_op jit(solution)/shard_map/atoms_tokens/pallas_call | solution.py:326
  30.4 0.0 copy-done
  30.4 0.9 %pair_add.1 = (bf16[8,256,128]{2,1,0:T(8,128)(2,1)}, bf16[128,128]{1,0:T(8,128)(2,1)}, bf16[2,384]{1,0:T(2,128)(2,1)}) custom-call(bf16[8,256,128]{2,1,0:T(8,128)(2,1)S(1)} %copy-done, f32[8,128]{1,0:T(8,128)S(1)} %get-tuple-element.10.rows, f32[256,128]{1,0:T(8,128)S(1)} %get-tuple-element.11.cols, bf16[128,128]{1,0:T(8,128)(2,1)S(1)} %get-tuple-element.12.atoms, ...), custom_call_target="tpu_custom_call" | custom-call | tf_op jit(solution)/shard_map/pair_add/pallas_call | solution.py:365
Async XLA Ops:
  0.6 29.7 %copy-start = (bf16[8,256,128]{2,1,0:T(8,128)(2,1)S(1)}, bf16[8,256,128]{2,1,0:T(8,128)(2,1)}, u32[]{:S(2)}) copy-start(bf16[8,256,128]{2,1,0:T(8,128)(2,1)} %pair.1) | copy-start | bytes 1572868

commit v9 on v8

--- a/solution.py
+++ b/solution.py
@@ -163,13 +163,13 @@
     barrier = pltpu.get_barrier_semaphore()
     for step in (-1, 1, 2):
         tell(barrier, along(step))
+    for d in NEAR:
+        tell(barrier, beside(d))
     for xs in range(NX):
         for c in range(2):
             pl.when(jnp.logical_not(home & (core == c) & (xs == x)))(
                 functools.partial(tell, barrier, device(x, z, c, xs))
             )
-    for d in NEAR:
-        tell(barrier, beside(d))
     for d in range(1, NX):
         tell(barrier, (wide, lax.rem(x + d, NX)))
 

time: 31.4 us -> 31.3 us (level)
  no operation moved by 1% of the time
where the time goes in v9:
time: 31.3 us; the launch traced here: 31.2 us
  Pallas kernels  30.5 us (97%)
  between operations  0.66 us (2%)
    pallas_call x1, Pallas kernels, on_device(): pl.pallas_call(functools.partial(kernel, 512 * ROWS), out_shape=[jax.Shap...  29.6 us
    pallas_call x1, Pallas kernels, on_device(): pl.pallas_call(finish, out_shape=[jax.ShapeDtypeStruct(pair_in.shape, bf1...  0.89 us

profile of v9, /device:TPU:4, one launch (start us, length us, event | category | flops | bytes accessed | tf_op | source)
XLA Modules:
  0.0 31.2 jit_solution(1236502523277663927)
XLA Ops:
  0.6 0.0 copy-start
  0.6 29.6 %atoms_tokens.1 = (bf16[128,128]{1,0:T(8,128)(2,1)S(1)}, bf16[2,384]{1,0:T(2,128)(2,1)S(1)}, f32[8,128]{1,0:T(8,128)S(1)}, f32[256,128]{1,0:T(8,128)S(1)}) custom-call(bf16[128,128]{1,0:T(8,128)(2,1)} %feats.1, s32[1,128]{1,0:T(1,128)} %bitcast.2, s32[1,4]{1,0:T(1,128)} %bitcast.3, bf16[2,128,384]{2,1,0:T(8,128)(2,1)} %w_qkv.1, bf16[2,128,128]{2,1,0:T(8,128)(2,1)} %w_out.1, ...), custom_call_target="tpu_custom_call" | custom-call | tf_op jit(solution)/shard_map/atoms_tokens/pallas_call | solution.py:326
  30.3 0.0 copy-done
  30.3 0.9 %pair_add.1 = (bf16[8,256,128]{2,1,0:T(8,128)(2,1)}, bf16[128,128]{1,0:T(8,128)(2,1)}, bf16[2,384]{1,0:T(2,128)(2,1)}) custom-call(bf16[8,256,128]{2,1,0:T(8,128)(2,1)S(1)} %copy-done, f32[8,128]{1,0:T(8,128)S(1)} %get-tuple-element.10.rows, f32[256,128]{1,0:T(8,128)S(1)} %get-tuple-element.11.cols, bf16[128,128]{1,0:T(8,128)(2,1)S(1)} %get-tuple-element.12.atoms, ...), custom_call_target="tpu_custom_call" | custom-call | tf_op jit(solution)/shard_map/pair_add/pallas_call | solution.py:365
Async XLA Ops:
  0.6 29.7 %copy-start = (bf16[8,256,128]{2,1,0:T(8,128)(2,1)S(1)}, bf16[8,256,128]{2,1,0:T(8,128)(2,1)}, u32[]{:S(2)}) copy-start(bf16[8,256,128]{2,1,0:T(8,128)(2,1)} %pair.1) | copy-start | bytes 1572868

commit v10 on v9

--- a/solution.py
+++ b/solution.py
@@ -126,10 +126,9 @@
 SPANS2 = [(64, 128), (192, 64)]
 
 
-def transform(pieces, own_proj, metas, base, n_atoms, wq, wo, wu, wd, between):
+def transform(pieces, rim, own_proj, metas, base, n_atoms, wq, wo, wu, wd, between):
     left, own, right, far = pieces
     biases = biases_of(metas, base, n_atoms)
-    rim = project(jnp.concatenate([left, right, far], axis=0), wq[0])
     proj = jnp.concatenate([rim[:ROWS], own_proj, rim[ROWS:]], axis=0)
     state = jnp.concatenate([left, own, right, far], axis=0)
     bias1 = [rows_of(biases[0], 192), rows_of(biases[1], 256), rows_of(biases[2], 256)]
@@ -217,14 +216,17 @@
     pl.semaphore_wait(around, len(NEAR))
     for d in (4, -4):
         tell(beyond.at[0 if d > 0 else 1], beside(d))
-    for s in sends:
+    for s in sends[:2]:
         s.wait_recv()
 
     metas = [halo[s, pl.ds(ROWS, 16)].astype(f32) for s in range(3)]
     ends = n_atoms // ROWS
     left = jnp.where(me == 0, 0.0, halo[0, pl.ds(0, ROWS)].astype(f32))
     right = jnp.where(me == ends - 1, 0.0, halo[2, pl.ds(0, ROWS)].astype(f32))
+    rim = project(jnp.concatenate([left, right], axis=0), wq[0])
+    sends[2].wait_recv()
     pieces = [left, own, right, jnp.where(me >= ends - 2, 0.0, far[...].astype(f32))]
+    rim = jnp.concatenate([rim, project(pieces[3], wq[0])], axis=0)
     match, counts = matches(metas[1], metas[2])
 
     near_side = (z > NZ // 2).astype(jnp.int32)
@@ -234,7 +236,7 @@
         tell(rest.at[which], beside(2 - 4 * which))
 
     state = transform(
-        pieces, own_proj, metas, me * ROWS, n_atoms, wq, wo, wu, wd,
+        pieces, rim, own_proj, metas, me * ROWS, n_atoms, wq, wo, wu, wd,
         functools.partial(pass_on, near_side),
     )
     atoms = state.astype(bf16)

time: 31.3 us -> 31.4 us (level)
  no operation moved by 1% of the time
where the time goes in v10:
time: 31.4 us; the launch traced here: 31 us
  Pallas kernels  30.3 us (96%)
  between operations  0.66 us (2%)
    pallas_call x1, Pallas kernels, on_device(): pl.pallas_call(functools.partial(kernel, 512 * ROWS), out_shape=[jax.Shap...  29.4 us
    pallas_call x1, Pallas kernels, on_device(): pl.pallas_call(finish, out_shape=[jax.ShapeDtypeStruct(pair_in.shape, bf1...  0.89 us

profile of v10, /device:TPU:4, one launch (start us, length us, event | category | flops | bytes accessed | tf_op | source)
XLA Modules:
  0.0 31.0 jit_solution(16511330549228848869)
XLA Ops:
  0.6 0.0 copy-start
  0.6 29.4 %atoms_tokens.1 = (bf16[128,128]{1,0:T(8,128)(2,1)S(1)}, bf16[2,384]{1,0:T(2,128)(2,1)S(1)}, f32[8,128]{1,0:T(8,128)S(1)}, f32[256,128]{1,0:T(8,128)S(1)}) custom-call(bf16[128,128]{1,0:T(8,128)(2,1)} %feats.1, s32[1,128]{1,0:T(1,128)} %bitcast.2, s32[1,4]{1,0:T(1,128)} %bitcast.3, bf16[2,128,384]{2,1,0:T(8,128)(2,1)} %w_qkv.1, bf16[2,128,128]{2,1,0:T(8,128)(2,1)} %w_out.1, ...), custom_call_target="tpu_custom_call" | custom-call | tf_op jit(solution)/shard_map/atoms_tokens/pallas_call | solution.py:328
  30.1 0.0 copy-done
  30.1 0.9 %pair_add.1 = (bf16[8,256,128]{2,1,0:T(8,128)(2,1)}, bf16[128,128]{1,0:T(8,128)(2,1)}, bf16[2,384]{1,0:T(2,128)(2,1)}) custom-call(bf16[8,256,128]{2,1,0:T(8,128)(2,1)S(1)} %copy-done, f32[8,128]{1,0:T(8,128)S(1)} %get-tuple-element.10.rows, f32[256,128]{1,0:T(8,128)S(1)} %get-tuple-element.11.cols, bf16[128,128]{1,0:T(8,128)(2,1)S(1)} %get-tuple-element.12.atoms, ...), custom_call_target="tpu_custom_call" | custom-call | tf_op jit(solution)/shard_map/pair_add/pallas_call | solution.py:367
Async XLA Ops:
  0.6 29.5 %copy-start = (bf16[8,256,128]{2,1,0:T(8,128)(2,1)S(1)}, bf16[8,256,128]{2,1,0:T(8,128)(2,1)}, u32[]{:S(2)}) copy-start(bf16[8,256,128]{2,1,0:T(8,128)(2,1)} %pair.1) | copy-start | bytes 1572868
